TPU v7x, 256 devices: a whole 4x4x8 slice. The times are simulated.
256 devices in a mesh: ctx: 16 (over x_lo, y, core), head: 16 (over z, x_hi).
Axes of the slice: x: 4 (x_hi: 2, x_lo: 2; x = x_hi * 2 + x_lo), y: 4, z: 8, core: 2. Of those that a mesh axis runs over, the one named last changes fastest.
Arguments:
- tokens: bfloat16 [16384, 5376], P('ctx', 'head'), may hold values from -48 to 48
- w_qkv: bfloat16 [5376, 8192], P('ctx', 'head')
Outputs:
- attended: bfloat16 [16384, 4096], P('ctx', 'head')
All inputs are finite; a program needn't handle non-finite values.
Results may differ from a plain program's by a relative error of at most 0.011.
Values may be sent and summed in bfloat16 or wider, within the bound.
No kernel may reach another device: no remote copies, remote signals or barrier semaphores. Data moves between devices by JAX's collectives and lax.ppermute only.
A program may use at most 128 MiB of HBM per device.

v0:
```python
import jax
import jax.numpy as jnp
from jax import lax
from jax.sharding import PartitionSpec as P

HEAD_DIM = 128
Q_PER_KV = 2
WINDOW = 1024


rope_base = 10000.0
query_scale = 168.0 ** (-0.5)
masked_score = -1e30


def passed_along(block, axis, distance):
    devices = range(lax.axis_size(axis))
    route = [(i - distance, i) for i in devices if i - distance in devices]
    return lax.ppermute(block, axis, route)


def rotate(projected, positions):
    head_width = projected.shape[-1]
    half_width = head_width // 2
    inverse = jnp.power(rope_base, -2.0 * jnp.arange(half_width, dtype=jnp.float32) / head_width)
    angles = positions.astype(jnp.float32)[:, None] * inverse[None, :]
    target_shape = (projected.shape[0],) + (1,) * (projected.ndim - 2) + (half_width,)
    cosine = jnp.cos(angles).reshape(target_shape)
    sine_part = jnp.sin(angles).reshape(target_shape)
    leading = projected[..., :half_width]
    second = projected[..., half_width:]
    return jnp.concatenate(
        [leading * cosine - second * sine_part, second * cosine + leading * sine_part], axis=-1
    )


def add_rows(left_rows, shard_rows):
    return jnp.dot(left_rows, shard_rows, preferred_element_type=jnp.float32)


def extend(key_rows, value_rows):
    stacked = jnp.stack([key_rows, value_rows], axis=0)
    border = passed_along(stacked, "ctx", 1)
    return (
        jnp.concatenate([border[0], key_rows], axis=0),
        jnp.concatenate([border[1], value_rows], axis=0),
    )


def attend(queries, key_rows, value_rows, key_anchor):
    row_count = queries.shape[0]
    block_rows = min(512, row_count)
    span = key_rows.shape[0] - row_count
    query_pos = jnp.arange(block_rows, dtype=jnp.int32)[:, None]
    key_pos = jnp.arange(block_rows + span, dtype=jnp.int32)[None, :]

    def one_block(block_index):
        first_row = block_index * block_rows
        query_block = lax.dynamic_slice_in_dim(queries, first_row, block_rows, 0)
        key_block = lax.dynamic_slice_in_dim(key_rows, first_row, block_rows + span, 0)
        value_block = lax.dynamic_slice_in_dim(value_rows, first_row, block_rows + span, 0)
        scores = (
            jnp.einsum("qkgd,ckd->kgqc", query_block, key_block, preferred_element_type=jnp.float32)
            * query_scale
        )
        allowed = (
            (key_pos > query_pos)
            & (key_pos <= query_pos + span)
            & (key_anchor + first_row + key_pos >= 0)
        )
        scores = jnp.where(allowed[None, None], scores, masked_score)
        highest = jnp.max(scores, axis=-1, keepdims=True)
        expanded = jnp.exp(scores - highest)
        probabilities = (expanded / jnp.sum(expanded, axis=-1, keepdims=True)).astype(jnp.bfloat16)
        summed = jnp.einsum(
            "kgqc,ckd->qkgd", probabilities, value_block, preferred_element_type=jnp.float32
        )
        return summed.astype(jnp.bfloat16)

    attended = lax.map(one_block, jnp.arange(row_count // block_rows, dtype=jnp.int32))
    return attended.reshape(row_count, -1)


def on_device(tokens, w_qkv):
    row_count = tokens.shape[0]
    groups = w_qkv.shape[1] // ((Q_PER_KV + 2) * HEAD_DIM)
    device_index = lax.axis_index("ctx")
    positions = device_index * row_count + jnp.arange(row_count, dtype=jnp.int32)
    key_anchor = device_index * row_count - WINDOW
    gathered = lax.all_gather(tokens, "head", axis=1, tiled=True)
    projected = add_rows(gathered, lax.all_gather(w_qkv, "ctx", axis=0, tiled=True))
    projected = projected.reshape(row_count, groups, Q_PER_KV + 2, HEAD_DIM)
    queries = rotate(projected[:, :, :Q_PER_KV], positions).astype(jnp.bfloat16)
    key_rows = rotate(projected[:, :, Q_PER_KV], positions).astype(jnp.bfloat16)
    value_rows = projected[:, :, Q_PER_KV + 1].astype(jnp.bfloat16)
    key_rows, value_rows = extend(key_rows, value_rows)
    return attend(queries, key_rows, value_rows, key_anchor)


def solution(mesh):
    placed = (P("ctx", "head"), P("ctx", "head"))
    return jax.shard_map(
        on_device, mesh=mesh, in_specs=placed, out_specs=P("ctx", "head"), check_vma=False
    )
```

profile of v0, /device:TPU:2, one launch (start us, length us, event | category | flops | bytes accessed | tf_op | source)
XLA Modules:
  0.0 274.9 jit_solution(17137558417569004634)
XLA Ops:
  6.5 0.0 all-gather.5.cloned.1.call-start
  6.5 0.7 all-gather.5.cloned.1.call-update
  7.3 0.0 all-gather.3.cloned.1.call-start
  7.3 0.7 all-gather.3.cloned.1.call-update
  8.1 3.1 %multiply_cosine_fusion = (f32[1024,64]{1,0:T(8,128)}, f32[1024,64]{1,0:T(8,128)}) fusion(f32[64]{0:T(128)S(1)} %multiply_power_fusion, f32[1024]{0:T(1024)S(1)} %add_convert_fusion.1), kind=kLoop, calls=%fused_computation.33 | loop fusion | flops 65536 | bytes 528640 | tf_op jit(solution)/shard_map/cos | solution.py:28
  11.1 43.1 %all-gather.5.cloned.1.call-done = bf16[5376,512]{1,0:T(8,128)(2,1)} async-done(((bf16[336,512]{1,0:T(8,128)(2,1)}), bf16[5376,512]{1,0:T(8,128)(2,1)}) %all-gather.5.cloned.1.call-update) | async-done | bytes 5505040 | tf_op jit(solution)/shard_map/all_gather | solution.py:91
  54.3 164.7 %all-gather.3.cloned.1.call-done = bf16[1024,5376]{0,1:T(8,128)(2,1)} async-done(((bf16[1024,336]{0,1:T(8,128)(2,1)}), bf16[1024,5376]{0,1:T(8,128)(2,1)}) %all-gather.3.cloned.1.call-update) | async-done | bytes 11010064 | tf_op jit(solution)/shard_map/all_gather | solution.py:90
  219.0 10.3 %fusion.37 = f32[1024,512]{0,1:T(8,128)S(1)} fusion(bf16[1024,5376]{0,1:T(8,128)(2,1)} %all-gather.3.cloned.1.call-done, bf16[5376,512]{1,0:T(8,128)(2,1)} %all-gather.5.cloned.1.call-done), kind=kOutput, calls=%fused_computation.56 | convolution fusion | flops 5637144576 | bytes 18612224 | tf_op jit(solution)/shard_map/dot_general | solution.py:38
  229.3 0.0 copy-start
  229.4 1.3 copy-done
  230.7 0.2 copy.21
  230.9 2.4 fusion.33
  233.3 0.2 copy.22
  233.5 1.0 pad_maximum_fusion
  234.4 2.1 collective-permute-start
  236.5 1.3 fusion.36
  237.8 0.3 copy.23
  238.1 0.3 copy.24
  238.5 1.5 subtract_convert_fusion
  240.0 0.3 pad_maximum_fusion.2
  240.3 7.1 %collective-permute-done = bf16[2,1024,1,128]{3,1,2,0:T(8,128)(2,1)} collective-permute-done((bf16[2,1024,1,128]{3,1,2,0:T(8,128)(2,1)}, bf16[2,1024,1,128]{3,1,2,0:T(8,128)(2,1)}, u32[]{:S(2)}, u32[]{:S(2)}) %collective-permute-start) | collective-permute-done | bytes 524320 | tf_op jit(solution)/shard_map/ppermute | solution.py:19
  247.3 1.1 slice_bitcast_fusion
  248.4 0.2 pad_maximum_fusion.1
  248.6 17.6 %while.12 = (s32[]{:T(128)}, bf16[2,512,1,2,128]{4,3,1,0,2:T(2,128)(2,1)}, s32[2]{0:T(128)S(1)}, bf16[2048,1,128]{2,0,1:T(8,128)(2,1)S(1)}, s32[]{:T(128)}, /*in...) while((s32[]{:T(128)}, ...), condition=%wide.region_3.4_spmd.clone.clone, body=%wide.region_0.3_spmd.clone.clone.sunk | while | flops 827459072 | bytes 28601632 | solution.py:80
  248.6 0.6 dynamic_slice.44
  249.9 1.3 fusion.50
  251.1 1.4 fusion.51
  252.5 1.4 fusion.52
  254.0 0.0 copy-start.1
  254.0 2.2 fusion.53
  256.2 0.2 copy.29
  256.3 0.0 copy-done.1
  256.4 0.2 constant_dynamic-update-slice_fusion.2
  256.6 0.0 copy-start.2
  256.6 0.8 copy-done.2
  257.4 0.6 dynamic_slice.44
  258.6 1.3 fusion.50
  259.9 1.4 fusion.51
  261.3 1.4 fusion.52
  262.7 0.0 copy-start.1
  262.8 2.2 fusion.53
  264.9 0.2 copy.29
  265.1 0.0 copy-done.1
  265.1 0.2 constant_dynamic-update-slice_fusion.2
  265.3 0.0 copy-start.2
  265.4 0.8 copy-done.2
  266.1 1.9 copy.27
  (10 shorter events, 0.1 us)
Async XLA Ops:
  6.5 47.7 %all-gather.5.cloned.1.call-start = ((), (), s32[]{:S(2)}) async-start(), calls=%async_computation.1 | async-start | bytes 5849088 | tf_op jit(solution)/shard_map/all_gather | solution.py:91
  7.3 211.7 %all-gather.3.cloned.1.call-start = ((), (), s32[]{:S(2)}) async-start(), calls=%async_computation | async-start | bytes 11698176 | tf_op jit(solution)/shard_map/all_gather | solution.py:90
  229.3 1.3 copy-start
  234.4 12.9 %collective-permute-start = (bf16[2,1024,1,128]{3,1,2,0:T(8,128)(2,1)}, bf16[2,1024,1,128]{3,1,2,0:T(8,128)(2,1)}, u32[]{:S(2)}, u32[]{:S(2)}) collective-permute-start(bf16[2,1024,1,128]{3,1,2,0:T(8,128)(2,1)} %pad_maximum_fusion), channel_id=1, source_target_pairs={{0,16},{16,32},{32,48},{48,64},{64,80},{80,96},{96,112},{112,128},... | collective-permute-start | bytes 1572872 | tf_op jit(solution)/shard_map/ppermute | solution.py:19
  254.0 2.4 copy-start.1
  256.6 0.8 copy-start.2
  262.7 2.4 copy-start.1
  265.3 0.8 copy-start.2
Sparse Core Ops, SparseCore 0:
  9.2 45.0 all-gather.4
  56.9 162.0 all-gather.2
where the time goes:
time: 275 us
  waiting for transfers between devices  216 us (79%)
  matrix products  17.5 us (6%)
  other arithmetic  13.8 us (5%)
  between operations  13.5 us (5%)
  local copies, waits for them, and re-layouts  10.1 us (4%)
    all_gather x1, waiting for transfers between devices, on_device(): gathered = lax.all_gather(tokens, 'head', axis=1, tiled=True)  165 us
    all_gather x1, waiting for transfers between devices, on_device(): lax.all_gather(w_qkv, 'ctx', axis=0, tiled=True)  43.1 us
    dot_general x1, matrix products, add_rows(): return jnp.dot(left_rows, shard_rows, preferred_element_type=jnp.float32)  10.3 us
    ppermute x1, waiting for transfers between devices, passed_along(): return lax.ppermute(block, axis, route)  7.08 us
  transfers between devices with their start and end apart: 3, of which 3 were waited for; matrix products, arithmetic and copies ran while one was open for 2% of the time, Pallas kernels for 0%

commit v1 on v0

v1 whole, which is shorter than its diff:
```python
import functools

import jax
import jax.numpy as jnp
from jax import lax
from jax.experimental import pallas as pl
from jax.experimental.pallas import tpu as pltpu
from jax.sharding import Mesh
from jax.sharding import PartitionSpec as P

HEAD = 128
Q_PER_KV = 2
WINDOW = 1024
ROPE_BASE = 10000.0
SCALE = 168.0 ** (-0.5)
LOG2E = 1.4426950408889634
MASKED = -1e30

AXES = ("x_lo", "y", "core", "z", "x_hi")
SIZES = (2, 4, 2, 8, 2)
CTX = ("x_lo", "y", "core")
HEADS = ("z", "x_hi")

CHUNKS = 2
TILE = 256
VMEM_BYTES = 40 * 1024 * 1024


def hop(block, axis, distance):
    n = lax.axis_size(axis)
    return lax.ppermute(block, axis, [(i, (i + distance) % n) for i in range(n)])


def swap(block, axis):
    return lax.ppermute(block, axis, [(0, 1), (1, 0)])


def ring_over_z(chunks):
    got = [[(0, chunk)] for chunk in chunks]
    forward, backward = list(chunks), list(chunks)
    for step in range(1, 5):
        for i in range(len(chunks)):
            if step < 4 or i % 2 == 0:
                forward[i] = hop(forward[i], "z", 1)
                got[i].append((-step, forward[i]))
            if step < 4 or i % 2 == 1:
                backward[i] = hop(backward[i], "z", -1)
                got[i].append((step, backward[i]))
    return got


def gather_weights(w):
    core, x_hi = lax.axis_index("core"), lax.axis_index("x_hi")
    crossed = lax.ppermute(w, ("core", "x_hi"), [(1, 2), (2, 1)])
    mine = jnp.where(core == x_hi, w, crossed)
    pair = jnp.stack([mine, swap(mine, "x_lo")])
    blocks = [pair] + [hop(pair, "y", d) for d in (1, 2, 3)]
    return blocks + [swap(b, "core") for b in blocks]


def product_kernel(distances, has_acc, where_ref, *refs):
    n = len(distances)
    tokens, weights = refs[:n], refs[n : n + 8]
    refs = refs[n + 8 :]
    acc_ref, refs = (refs[0], refs[1:]) if has_acc else (None, refs)
    out_ref, tok, wts, tok_sem, wts_sem = refs
    depth = tokens[0].shape[0]
    case = where_ref[0]
    for j in range(n):
        pltpu.make_async_copy(tokens[j], tok.at[pl.ds(j * depth, depth)], tok_sem.at[j]).start()
    for half in range(2):
        for k in range(4):

            @pl.when(case == half * 4 + k)
            def _(half=half, k=k):
                for j, d in enumerate(distances):
                    source = weights[half * 4 + (k - d) % 4].at[where_ref[1 + d % 8]]
                    pltpu.make_async_copy(
                        source, wts.at[pl.ds(j * depth, depth)], wts_sem.at[j]
                    ).start()

    for j in range(n):
        pltpu.make_async_copy(tokens[j], tok.at[pl.ds(j * depth, depth)], tok_sem.at[j]).wait()
        pltpu.make_async_copy(
            weights[0].at[0], wts.at[pl.ds(j * depth, depth)], wts_sem.at[j]
        ).wait()
    total = lax.dot_general(
        tok[...], wts[...], (((0,), (0,)), ((), ())), preferred_element_type=jnp.float32
    )
    if has_acc:
        total = total + acc_ref[...]
    out_ref[...] = total.astype(out_ref.dtype)


def product(where, shards, weights, acc, dtype):
    distances = tuple(d for d, _ in shards)
    tokens = [t for _, t in shards]
    depth, rows = tokens[0].shape
    columns = weights[0].shape[-1]
    n = len(tokens)
    hbm = pl.BlockSpec(memory_space=pl.ANY)
    vmem = pl.BlockSpec(memory_space=pltpu.VMEM)
    operands = [where, *tokens, *weights]
    specs = [pl.BlockSpec(memory_space=pltpu.SMEM)] + [hbm] * (n + 8)
    if acc is not None:
        operands.append(acc)
        specs.append(vmem)
    return pl.pallas_call(
        functools.partial(product_kernel, distances, acc is not None),
        out_shape=jax.ShapeDtypeStruct((rows, columns), dtype),
        in_specs=specs,
        out_specs=vmem,
        scratch_shapes=[
            pltpu.VMEM((n * depth, rows), jnp.bfloat16),
            pltpu.VMEM((n * depth, columns), jnp.bfloat16),
            pltpu.SemaphoreType.DMA((n,)),
            pltpu.SemaphoreType.DMA((n,)),
        ],
        compiler_params=pltpu.CompilerParams(vmem_limit_bytes=VMEM_BYTES),
        cost_estimate=pl.CostEstimate(
            flops=2 * n * depth * rows * columns,
            bytes_accessed=2 * n * depth * (rows + columns) + 4 * rows * columns,
            transcendentals=0,
        ),
    )(*operands)


def finish_kernel(keep_ref, sent_ref, cos_ref, sin_ref, q_ref, kv_ref):
    cos, sin = cos_ref[...], sin_ref[...]
    for j in range(4):
        columns = pl.ds(j * HEAD, HEAD)
        block = keep_ref[:, columns] + sent_ref[:, columns].astype(jnp.float32)
        if j < 3:
            block = block * cos + pltpu.roll(block, HEAD // 2, 1) * sin
        block = block.astype(jnp.bfloat16)
        if j < 2:
            q_ref[:, columns] = block
        else:
            kv_ref[:, pl.ds((j - 2) * HEAD, HEAD)] = block


def finish(keep, sent, cos, sin):
    rows = keep.shape[0]
    vmem = pl.BlockSpec(memory_space=pltpu.VMEM)
    return pl.pallas_call(
        finish_kernel,
        out_shape=[jax.ShapeDtypeStruct((rows, 2 * HEAD), jnp.bfloat16)] * 2,
        in_specs=[vmem] * 4,
        out_specs=[vmem] * 2,
        compiler_params=pltpu.CompilerParams(vmem_limit_bytes=VMEM_BYTES),
        cost_estimate=pl.CostEstimate(
            flops=rows * 2048, bytes_accessed=rows * 6000, transcendentals=0
        ),
    )(keep, sent, cos, sin)


def attend_kernel(chunks, first_ref, *refs):
    q_refs, own_refs, before_refs = refs[:chunks], refs[chunks : 2 * chunks], refs[2 * chunks : 3 * chunks]
    out_ref = refs[3 * chunks]
    rows = q_refs[0].shape[0]
    per_chunk = rows // TILE
    tiles = chunks * per_chunk
    outside = jnp.where(first_ref[0] == 0, jnp.float32(MASKED), jnp.float32(0))
    row = lax.broadcasted_iota(jnp.int32, (2 * TILE, TILE), 0) % TILE
    column = lax.broadcasted_iota(jnp.int32, (2 * TILE, TILE), 1)
    later = column > row

    def piece(group, tile, start):
        ref = group[tile // per_chunk]
        return ref[pl.ds(tile % per_chunk * TILE, TILE), pl.ds(start, HEAD)]

    for i in range(tiles):
        q = jnp.concatenate([piece(q_refs, i, 0), piece(q_refs, i, HEAD)], axis=0)
        scores = []
        for t in range(tiles + 1):
            source, tile = (before_refs, i + t) if i + t < tiles else (own_refs, i + t - tiles)
            s = lax.dot_general(
                q,
                piece(source, tile, 0),
                (((1,), (1,)), ((), ())),
                preferred_element_type=jnp.float32,
            )
            if i + t < tiles:
                s = s + outside
            if t == 0:
                s = jnp.where(later, s, MASKED)
            if t == tiles:
                s = jnp.where(later, MASKED, s)
            scores.append(s)
        highest = functools.reduce(jnp.maximum, scores)
        highest = jnp.max(highest, axis=-1, keepdims=True)
        shift = highest * (SCALE * LOG2E)
        total, summed = None, None
        for t in range(tiles + 1):
            source, tile = (before_refs, i + t) if i + t < tiles else (own_refs, i + t - tiles)
            p = jnp.exp2(scores[t] * (SCALE * LOG2E) - shift)
            total = p if total is None else total + p
            part = jnp.dot(
                p.astype(jnp.bfloat16),
                piece(source, tile, HEAD),
                preferred_element_type=jnp.float32,
            )
            summed = part if summed is None else summed + part
        total = jnp.sum(total, axis=-1, keepdims=True)
        out = (summed / total).astype(jnp.bfloat16)
        out_ref[pl.ds(i * TILE, TILE), pl.ds(0, HEAD)] = out[:TILE]
        out_ref[pl.ds(i * TILE, TILE), pl.ds(HEAD, HEAD)] = out[TILE:]


def attend(first, queries, own, before):
    chunks = len(queries)
    rows = queries[0].shape[0]
    vmem = pl.BlockSpec(memory_space=pltpu.VMEM)
    return pl.pallas_call(
        functools.partial(attend_kernel, chunks),
        out_shape=jax.ShapeDtypeStruct((chunks * rows, 2 * HEAD), jnp.bfloat16),
        in_specs=[pl.BlockSpec(memory_space=pltpu.SMEM)] + [vmem] * (3 * chunks),
        out_specs=vmem,
        compiler_params=pltpu.CompilerParams(vmem_limit_bytes=VMEM_BYTES),
        cost_estimate=pl.CostEstimate(
            flops=2 * 2 * 2 * chunks * rows * (WINDOW + TILE) * HEAD,
            bytes_accessed=chunks * rows * 2048,
            transcendentals=2 * chunks * rows * (WINDOW + TILE),
        ),
    )(first, *queries, *own, *before)


def rotary_tables(positions):
    half = HEAD // 2
    inverse = jnp.power(ROPE_BASE, -2.0 * jnp.arange(half, dtype=jnp.float32) / HEAD)
    angles = positions.astype(jnp.float32)[:, None] * inverse[None, :]
    cos, sin = jnp.cos(angles), jnp.sin(angles)
    return jnp.concatenate([cos, cos], axis=1), jnp.concatenate([-sin, sin], axis=1)


def on_device(tokens, w_qkv):
    row_count = tokens.shape[0]
    rows = row_count // CHUNKS
    x_lo, y, core, z, x_hi = (lax.axis_index(a) for a in AXES)
    ctx = (x_lo * 4 + y) * 2 + core
    positions = ctx * row_count + jnp.arange(row_count, dtype=jnp.int32)
    cos, sin = rotary_tables(positions)

    away = (z + jnp.arange(8, dtype=jnp.int32)) % 8
    x_rel = (x_lo + away // 4) % 2
    keep_half = jnp.where(core == x_hi, 0, 1)
    y_rel = (y - z) % 4

    def where(half):
        return jnp.concatenate([(half * 4 + y_rel)[None], x_rel]).astype(jnp.int32)

    keep_where, send_where = where(keep_half), where(1 - keep_half)

    shards = ring_over_z([tokens[i * rows : (i + 1) * rows].T for i in range(CHUNKS)])
    weights = gather_weights(w_qkv)

    queries, own, before = [], [], []
    for i in range(CHUNKS):
        early, late = shards[i][:5], shards[i][5:]
        send = product(send_where, early, weights, None, jnp.float32)
        keep = product(keep_where, early, weights, None, jnp.float32)
        send = product(send_where, late, weights, send, jnp.bfloat16)
        sent = swap(send, "x_hi")
        keep = product(keep_where, late, weights, keep, jnp.float32)
        span = slice(i * rows, (i + 1) * rows)
        q, kv = finish(keep, sent, cos[span], sin[span])
        queries.append(q)
        own.append(kv)
        before.append(lax.ppermute(kv, CTX, [(c, c + 1) for c in range(15)]))
    return attend(ctx.astype(jnp.int32)[None], queries, own, before)


def solution(mesh):
    fine = Mesh(mesh.devices.reshape(SIZES), AXES)
    placed = P(CTX, HEADS)
    return jax.shard_map(
        on_device, mesh=fine, in_specs=(placed, placed), out_specs=placed, check_vma=False
    )
```

time: 275 us -> 127 us (0.46)
  waiting for transfers between devices: 216 us -> 37.2 us
  starting transfers between devices: 2.13 us -> 46.6 us
  Pallas kernels: 0 us -> 30 us
  matrix products: 17.5 us -> 0 us
  between operations: 13.5 us -> 0.34 us
  other arithmetic: 13.8 us -> 2.45 us
    all_gather x2 -> x0, waiting for transfers between devices: 208 us -> none  [the longest x1 165 us: on_device(): gathered = lax.all_gather(tokens, 'head', axis=1, tiled=True)]
    ppermute x1 -> x27, starting transfers between devices: 2.09 us -> 46.6 us  [the longest x17 28.6 us: hop(): lax.ppermute(block, axis, [(i, (i + distance) % n) for i in range(n)])]
    ppermute x1 -> x27, waiting for transfers between devices: 7.08 us -> 37.2 us  [the longest x17 30.6 us: hop(): lax.ppermute(block, axis, [(i, (i + distance) % n) for i in range(n)])]
    pallas_call x0 -> x11, Pallas kernels: none -> 30 us  [the longest x8 24.3 us: product(): pl.pallas_call(functools.partial(product_kernel, distances, acc is not No...]
    dot_general x5 -> x0, matrix products: 17.5 us -> none  [the longest x1 10.3 us: add_rows(): return jnp.dot(left_rows, shard_rows, preferred_element_type=jnp.float32)]
    another operation x3 -> x1, other arithmetic: 4.85 us -> 0.06 us  [gather_weights(): pair = jnp.stack([mine, swap(mine, 'x_lo')])]
    cos x1 -> x0, other arithmetic: 3.08 us -> none  [rotate(): cosine = jnp.cos(angles).reshape(target_shape)]
    reduce_sum x2 -> x0, other arithmetic: 2.88 us -> none  [one_block(): jnp.sum(expanded, axis=-1, keepdims=True)]
  transfers between devices with their start and end apart: 3 -> 27, of which waited for: 3 -> 9; matrix products, arithmetic and copies ran while one was open for 2% -> 3% of each run, Pallas kernels for 0% -> 20%
where the time goes in v1:
time: 127 us; the launch traced here: 125 us
  starting transfers between devices  46.6 us (37%)
  waiting for transfers between devices  37.2 us (29%)
  Pallas kernels  30 us (24%)
  local copies, waits for them, and re-layouts  8.21 us (6%)
  other arithmetic  2.45 us (2%)
    ppermute x17, waiting for transfers between devices, hop(): lax.ppermute(block, axis, [(i, (i + distance) % n) for i in range(n)])  30.6 us
    ppermute x17, starting transfers between devices, hop(): lax.ppermute(block, axis, [(i, (i + distance) % n) for i in range(n)])  28.6 us
    pallas_call x8, Pallas kernels, product(): pl.pallas_call(functools.partial(product_kernel, distances, acc is not No...  24.3 us
    ppermute x7, starting transfers between devices, swap(): return lax.ppermute(block, axis, [(0, 1), (1, 0)])  11.5 us
    unnamed x38, local copies, waits for them, and re-layouts  7.08 us
    ppermute x2, waiting for transfers between devices, on_device(): before.append(lax.ppermute(kv, CTX, [(c, c + 1) for c in range(15)]))  6.6 us
    ppermute x2, starting transfers between devices, on_device(): before.append(lax.ppermute(kv, CTX, [(c, c + 1) for c in range(15)]))  5.65 us
    pallas_call x1, Pallas kernels, attend(): pl.pallas_call(functools.partial(attend_kernel, chunks), out_shape=jax.Sh...  5.09 us
  transfers between devices with their start and end apart: 27, of which 9 were waited for; matrix products, arithmetic and copies ran while one was open for 3% of the time, Pallas kernels for 20%

profile of v1, /device:TPU:2, one launch (start us, length us, event | category | flops | bytes accessed | tf_op | source)
XLA Modules:
  0.0 124.8 jit_solution(10075907635062973702)
XLA Ops:
  0.0 0.8 collective-permute-start.7
  0.8 1.1 slice_bitcast_fusion
  2.0 0.0 copy-start
  2.0 2.0 %collective-permute-start.17 = (bf16[336,512]{1,0:T(8,128)(2,1)S(1)}, bf16[336,512]{1,0:T(8,128)(2,1)S(1)}, u32[]{:S(2)}, u32[]{:S(2)}) collective-permute-start(bf16[336,512]{1,0:T(8,128)(2,1)S(1)} %get-tuple-element.15.refs_0_), channel_id=1, source_target_pairs={{0,2},{2,4},{4,6},{6,8},{8,10},{10,12},{12,14},{14,0},{1,3},{3,5},... | collective-permute-start | bytes 1032200 | tf_op jit(solution)/shard_map/ppermute | solution.py:31
  4.0 4.0 %collective-permute-start.20 = (bf16[336,512]{1,0:T(8,128)(2,1)S(1)}, bf16[336,512]{1,0:T(8,128)(2,1)S(1)}, u32[]{:S(2)}, u32[]{:S(2)}) collective-permute-start(bf16[336,512]{1,0:T(8,128)(2,1)S(1)} %get-tuple-element.15.refs_0_), channel_id=1, source_target_pairs={{0,14},{2,0},{4,2},{6,4},{8,6},{10,8},{12,10},{14,12},{1,15},{3,1}... | collective-permute-start | bytes 1032200 | tf_op jit(solution)/shard_map/ppermute | solution.py:31
  8.0 0.6 collective-permute-start.8
  8.7 3.2 %collective-permute-start.3 = (bf16[336,512]{1,0:T(8,128)(2,1)S(1)}, bf16[336,512]{1,0:T(8,128)(2,1)S(1)}, u32[]{:S(2)}, u32[]{:S(2)}) collective-permute-start(bf16[336,512]{1,0:T(8,128)(2,1)S(1)} %get-tuple-element.16.refs_0_), channel_id=1, source_target_pairs={{0,14},{2,0},{4,2},{6,4},{8,6},{10,8},{12,10},{14,12},{1,15},{3,1}... | collective-permute-start | bytes 1032200 | tf_op jit(solution)/shard_map/ppermute | solution.py:31
  11.9 2.1 %collective-permute-done.17.refs_1_ = bf16[336,512]{1,0:T(8,128)(2,1)S(1)} collective-permute-done((bf16[336,512]{1,0:T(8,128)(2,1)S(1)}, bf16[336,512]{1,0:T(8,128)(2,1)S(1)}, u32[]{:S(2)}, u32[]{:S(2)}) %collective-permute-start.17) | collective-permute-done | bytes 344096 | tf_op jit(solution)/shard_map/ppermute | solution.py:31
  14.0 0.0 collective-permute-start.18
  14.0 3.6 %collective-permute-start.21 = (bf16[336,512]{1,0:T(8,128)(2,1)S(1)}, bf16[336,512]{1,0:T(8,128)(2,1)S(1)}, u32[]{:S(2)}, u32[]{:S(2)}) collective-permute-start(bf16[336,512]{1,0:T(8,128)(2,1)S(1)} %collective-permute-done.20.refs_2_), channel_id=1, source_target_pairs={{0,14},{2,0},{4,2},{6,4},{8,6},{10,8},{12,10},{14,12},{1,15},{3,1}... | collective-permute-start | bytes 1032200 | tf_op jit(solution)/shard_map/ppermute | solution.py:31
  17.6 0.1 pad_maximum_fusion.refs_5_.refs_3_
  17.7 1.7 %collective-permute-start.9 = (bf16[2,336,512]{2,1,0:T(8,128)(2,1)S(1)}, bf16[2,336,512]{2,1,0:T(8,128)(2,1)S(1)}, u32[]{:S(2)}, u32[]{:S(2)}) collective-permute-start(bf16[2,336,512]{2,1,0:T(8,128)(2,1)S(1)} %pad_maximum_fusion.refs_5_.refs_3_), channel_id=1, source_target_pairs={{0,32},{32,64},{64,96},{96,0},{1,33},{33,65},{65,97},{97,1},{2,34}... | collective-permute-start | bytes 2064392 | tf_op jit(solution)/shard_map/ppermute | solution.py:31
  19.3 1.2 collective-permute-done.refs_1_
  20.5 3.2 %collective-permute-start.10 = (bf16[2,336,512]{2,1,0:T(8,128)(2,1)S(1)}, bf16[2,336,512]{2,1,0:T(8,128)(2,1)S(1)}, u32[]{:S(2)}, u32[]{:S(2)}) collective-permute-start(bf16[2,336,512]{2,1,0:T(8,128)(2,1)S(1)} %pad_maximum_fusion.refs_5_.refs_3_), channel_id=1, source_target_pairs={{0,64},{32,96},{64,0},{96,32},{1,65},{33,97},{65,1},{97,33},{2,66}... | collective-permute-start | bytes 2064392 | tf_op jit(solution)/shard_map/ppermute | solution.py:31
  23.7 1.1 collective-permute-start.11
  24.8 2.8 %collective-permute-done.18.refs_3_ = bf16[336,512]{1,0:T(8,128)(2,1)} collective-permute-done((bf16[336,512]{1,0:T(8,128)(2,1)S(1)}, bf16[336,512]{1,0:T(8,128)(2,1)}, u32[]{:S(2)}, u32[]{:S(2)}) %collective-permute-start.18) | collective-permute-done | bytes 344096 | tf_op jit(solution)/shard_map/ppermute | solution.py:31
  27.5 0.0 collective-permute-start.1
  27.5 0.7 copy-done.11
  28.3 0.0 collective-permute-done.21.refs_4_
  28.3 3.2 %collective-permute-start.4 = (bf16[336,512]{1,0:T(8,128)(2,1)S(1)}, bf16[336,512]{1,0:T(8,128)(2,1)}, u32[]{:S(2)}, u32[]{:S(2)}) collective-permute-start(bf16[336,512]{1,0:T(8,128)(2,1)S(1)} %collective-permute-done.3.refs_2_), channel_id=1, source_target_pairs={{0,14},{2,0},{4,2},{6,4},{8,6},{10,8},{12,10},{14,12},{1,15},{3,1}... | collective-permute-start | bytes 1032200 | tf_op jit(solution)/shard_map/ppermute | solution.py:31
  31.5 0.7 copy-done.13
  32.2 4.3 %collective-permute-done.1.refs_3_ = bf16[336,512]{1,0:T(8,128)(2,1)} collective-permute-done((bf16[336,512]{1,0:T(8,128)(2,1)S(1)}, bf16[336,512]{1,0:T(8,128)(2,1)}, u32[]{:S(2)}, u32[]{:S(2)}) %collective-permute-start.1) | collective-permute-done | bytes 344096 | tf_op jit(solution)/shard_map/ppermute | solution.py:31
  36.5 1.4 %collective-permute-start.22 = (bf16[336,512]{1,0:T(8,128)(2,1)S(1)}, bf16[336,512]{1,0:T(8,128)(2,1)}, u32[]{:S(2)}, u32[]{:S(2)}) collective-permute-start(bf16[336,512]{1,0:T(8,128)(2,1)S(1)} %collective-permute-done.21.refs_4_), channel_id=1, source_target_pairs={{0,14},{2,0},{4,2},{6,4},{8,6},{10,8},{12,10},{14,12},{1,15},{3,1}... | collective-permute-start | bytes 1032200 | tf_op jit(solution)/shard_map/ppermute | solution.py:31
  37.9 0.7 copy-done.15
  38.7 2.9 %collective-permute-start.12 = (bf16[2,336,512]{2,1,0:T(8,128)(2,1)S(1)}, bf16[2,336,512]{2,1,0:T(8,128)(2,1)S(1)}, u32[]{:S(2)}, u32[]{:S(2)}) collective-permute-start(bf16[2,336,512]{2,1,0:T(8,128)(2,1)S(1)} %pad_maximum_fusion.refs_5_.refs_3_), channel_id=1, source_target_pairs={{0,16},{16,0},{1,17},{17,1},{2,18},{18,2},{3,19},{19,3},{4,20},{20... | collective-permute-start | bytes 2064392 | tf_op jit(solution)/shard_map/ppermute | solution.py:35
  41.5 0.1 collective-permute-start.13
  41.6 7.6 %collective-permute-done.10.refs_7_.refs_5_ = bf16[2,336,512]{2,1,0:T(8,128)(2,1)S(1)} collective-permute-done((bf16[2,336,512]{2,1,0:T(8,128)(2,1)S(1)}, bf16[2,336,512]{2,1,0:T(8,128)(2,1)S(1)}, u32[]{:S(2)}, u32[]{:S(2)}) %collective-permute-start.10) | collective-permute-done | bytes 688160 | tf_op jit(solution)/shard_map/ppermute | solution.py:31
  49.2 3.9 %collective-permute-start.14 = (bf16[2,336,512]{2,1,0:T(8,128)(2,1)S(1)}, bf16[2,336,512]{2,1,0:T(8,128)(2,1)}, u32[]{:S(2)}, u32[]{:S(2)}) collective-permute-start(bf16[2,336,512]{2,1,0:T(8,128)(2,1)S(1)} %collective-permute-done.10.refs_7_.refs_5_), channel_id=1, source_target_pairs={{0,16},{16,0},{1,17},{17,1},{2,18},{18,2},{3,19},{19,3},{4,20},{20... | collective-permute-start | bytes 2064392 | tf_op jit(solution)/shard_map/ppermute | solution.py:35
  53.1 1.2 collective-permute-done.11.refs_8_.refs_6_
  54.3 1.0 collective-permute-start.15
  55.3 0.0 collective-permute-start.2
  55.3 11.5 %collective-permute-done.2.refs_0_ = bf16[336,512]{1,0:T(8,128)(2,1)} collective-permute-done((bf16[336,512]{1,0:T(8,128)(2,1)}, bf16[336,512]{1,0:T(8,128)(2,1)}, u32[]{:S(2)}, u32[]{:S(2)}) %collective-permute-start.2) | collective-permute-done | bytes 344096 | tf_op jit(solution)/shard_map/ppermute | solution.py:31
  66.8 3.2 %collective-permute-start.23 = (bf16[336,512]{1,0:T(8,128)(2,1)}, bf16[336,512]{1,0:T(8,128)(2,1)}, u32[]{:S(2)}, u32[]{:S(2)}) collective-permute-start(bf16[336,512]{1,0:T(8,128)(2,1)} %collective-permute-done.22.refs_1_), channel_id=1, source_target_pairs={{0,14},{2,0},{4,2},{6,4},{8,6},{10,8},{12,10},{14,12},{1,15},{3,1}... | collective-permute-start | bytes 1032200 | tf_op jit(solution)/shard_map/ppermute | solution.py:31
  70.0 0.1 pad_add_fusion.1
  70.1 0.0 collective-permute-start.5
  70.1 2.0 %collective-permute-start.6 = (bf16[336,512]{1,0:T(8,128)(2,1)}, bf16[336,512]{1,0:T(8,128)(2,1)}, u32[]{:S(2)}, u32[]{:S(2)}) collective-permute-start(bf16[336,512]{1,0:T(8,128)(2,1)} %collective-permute-done.2.refs_0_), channel_id=1, source_target_pairs={{0,2},{2,4},{4,6},{6,8},{8,10},{10,12},{12,14},{14,0},{1,3},{3,5},... | collective-permute-start | bytes 1032200 | tf_op jit(solution)/shard_map/ppermute | solution.py:31
  72.2 1.0 copy-done.3
  73.1 1.0 copy-done.6
  74.1 1.0 copy-done.9
  75.1 1.0 copy-done.16
  76.1 3.7 %shard_map.35.refs_11_ = f32[512,512]{1,0:T(8,128)S(1)} custom-call(s32[9]{0:T(128)S(1)} %get-tuple-element.22.where_ref, bf16[336,512]{1,0:T(8,128)(2,1)S(1)} %copy-done.3, bf16[336,512]{1,0:T(8,128)(2,1)S(1)} %copy-done.6, bf16[336,512]{1,0:T(8,128)(2,1)S(1)} %copy-done.9, bf16[336,512]{1,0:T(8,128)(2,1)} %collective-permute-done.18.refs_3_, ...), custom_call_target="tpu_custom_call" | custom-call | flops 880803840 | bytes 4489216 | tf_op jit(solution)/shard_map/pallas_call | solution.py:108
  79.8 0.0 copy-start.1
  79.9 2.7 %shard_map.36 = bf16[512,512]{1,0:T(8,128)(2,1)S(1)} custom-call(s32[9]{0:T(128)S(1)} %get-tuple-element.22.where_ref, bf16[336,512]{1,0:T(8,128)(2,1)} %collective-permute-done.19.refs_0_, bf16[336,512]{1,0:T(8,128)(2,1)} %collective-permute-done.22.refs_1_, bf16[336,512]{1,0:T(8,128)(2,1)} %collective-permute-done.23.refs_2_, ...), custom_call_target="tpu_custom_call" | custom-call | flops 528482304 | bytes 3112960 | tf_op jit(solution)/shard_map/pallas_call | solution.py:108
  82.6 0.1 collective-permute-start.24
  82.7 3.7 %shard_map.30.refs_11_ = f32[512,512]{1,0:T(8,128)S(1)} custom-call(s32[9]{0:T(128)S(1)} %get-tuple-element.22.where_ref, bf16[336,512]{1,0:T(8,128)(2,1)S(1)} %copy-done.1, bf16[336,512]{1,0:T(8,128)(2,1)S(1)} %copy-done.12, bf16[336,512]{1,0:T(8,128)(2,1)S(1)} %copy-done.14, bf16[336,512]{1,0:T(8,128)(2,1)} %collective-permute-done.1.refs_3_, ...), custom_call_target="tpu_custom_call" | custom-call | flops 880803840 | bytes 4489216 | tf_op jit(solution)/shard_map/pallas_call | solution.py:108
  86.4 2.7 %shard_map.31 = bf16[512,512]{1,0:T(8,128)(2,1)S(1)} custom-call(s32[9]{0:T(128)S(1)} %get-tuple-element.22.where_ref, bf16[336,512]{1,0:T(8,128)(2,1)} %collective-permute-done.2.refs_0_, bf16[336,512]{1,0:T(8,128)(2,1)} %collective-permute-done.5.refs_1_, bf16[336,512]{1,0:T(8,128)(2,1)} %collective-permute-done.6.refs_2_, ...), custom_call_target="tpu_custom_call" | custom-call | flops 528482304 | bytes 3112960 | tf_op jit(solution)/shard_map/pallas_call | solution.py:108
  89.2 2.9 %collective-permute-start.16 = (bf16[512,512]{1,0:T(8,128)(2,1)S(1)}, bf16[512,512]{1,0:T(8,128)(2,1)S(1)}, u32[]{:S(2)}, u32[]{:S(2)}) collective-permute-start(bf16[512,512]{1,0:T(8,128)(2,1)S(1)} %shard_map.31), channel_id=1, source_target_pairs={{0,1},{1,0},{2,3},{3,2},{4,5},{5,4},{6,7},{7,6},{8,9},{9,8},{10,11... | collective-permute-start | bytes 1572872 | tf_op jit(solution)/shard_map/ppermute | solution.py:35
  92.1 1.9 %multiply_sine_fusion = (f32[1024,64]{1,0:T(8,128)S(1)}, f32[1024,64]{1,0:T(8,128)S(1)}, f32[1024,64]{1,0:T(8,128)S(1)}) fusion(f32[64]{0:T(128)S(1)} %multiply_power_fusion, f32[1024]{0:T(1024)S(1)} %add_convert_fusion), kind=kLoop, calls=%fused_computation | loop fusion | flops 131072 | bytes 790784 | tf_op jit(solution)/shard_map/sin | solution.py:232
  94.0 0.3 pad_maximum_fusion.1
  94.4 0.6 copy-done.4
  95.0 0.1 copy-done.7
  95.1 0.1 copy-done.10
  95.2 0.1 copy-done.17
  95.3 3.2 %shard_map.33.refs_11_ = f32[512,512]{1,0:T(8,128)S(1)} custom-call(s32[9]{0:T(128)S(1)} %get-tuple-element.23.where_ref, bf16[336,512]{1,0:T(8,128)(2,1)S(1)} %copy-done.4, bf16[336,512]{1,0:T(8,128)(2,1)S(1)} %copy-done.7, bf16[336,512]{1,0:T(8,128)(2,1)S(1)} %copy-done.10, bf16[336,512]{1,0:T(8,128)(2,1)} %collective-permute-done.18.refs_3_, ...), custom_call_target="tpu_custom_call" | custom-call | flops 880803840 | bytes 4489216 | tf_op jit(solution)/shard_map/pallas_call | solution.py:108
  98.5 2.5 %shard_map.34.keep_ref = f32[512,512]{1,0:T(8,128)S(1)} custom-call(s32[9]{0:T(128)S(1)} %get-tuple-element.23.where_ref, bf16[336,512]{1,0:T(8,128)(2,1)} %collective-permute-done.19.refs_0_, bf16[336,512]{1,0:T(8,128)(2,1)} %collective-permute-done.22.refs_1_, bf16[336,512]{1,0:T(8,128)(2,1)} %collective-permute-done.23.refs_2_, ...), custom_call_target="tpu_custom_call" | custom-call | flops 528482304 | bytes 3112960 | tf_op jit(solution)/shard_map/pallas_call | solution.py:108
  101.0 3.2 %shard_map.28.refs_11_ = f32[512,512]{1,0:T(8,128)S(1)} custom-call(s32[9]{0:T(128)S(1)} %get-tuple-element.23.where_ref, bf16[336,512]{1,0:T(8,128)(2,1)S(1)} %copy-done.1, bf16[336,512]{1,0:T(8,128)(2,1)S(1)} %copy-done.12, bf16[336,512]{1,0:T(8,128)(2,1)S(1)} %copy-done.14, bf16[336,512]{1,0:T(8,128)(2,1)} %collective-permute-done.1.refs_3_, ...), custom_call_target="tpu_custom_call" | custom-call | flops 880803840 | bytes 4489216 | tf_op jit(solution)/shard_map/pallas_call | solution.py:108
  104.2 2.5 %shard_map.29.keep_ref = f32[512,512]{1,0:T(8,128)S(1)} custom-call(s32[9]{0:T(128)S(1)} %get-tuple-element.23.where_ref, bf16[336,512]{1,0:T(8,128)(2,1)} %collective-permute-done.2.refs_0_, bf16[336,512]{1,0:T(8,128)(2,1)} %collective-permute-done.5.refs_1_, bf16[336,512]{1,0:T(8,128)(2,1)} %collective-permute-done.6.refs_2_, ...), custom_call_target="tpu_custom_call" | custom-call | flops 528482304 | bytes 3112960 | tf_op jit(solution)/shard_map/pallas_call | solution.py:108
  106.8 0.3 shard_map.37
  107.1 1.9 %collective-permute-start.26 = (bf16[512,256]{1,0:T(8,128)(2,1)S(1)}, bf16[512,256]{1,0:T(8,128)(2,1)S(1)}, u32[]{:S(2)}, u32[]{:S(2)}) collective-permute-start(bf16[512,256]{1,0:T(8,128)(2,1)S(1)} %get-tuple-element.12.refs_3_), channel_id=1, source_target_pairs={{0,16},{16,32},{32,48},{48,64},{64,80},{80,96},{96,112},{112,128},... | collective-permute-start | bytes 786440 | tf_op jit(solution)/shard_map/ppermute | solution.py:269
  109.0 0.3 shard_map.32
  109.4 3.7 %collective-permute-start.25 = (bf16[512,256]{1,0:T(8,128)(2,1)S(1)}, bf16[512,256]{1,0:T(8,128)(2,1)S(1)}, u32[]{:S(2)}, u32[]{:S(2)}) collective-permute-start(bf16[512,256]{1,0:T(8,128)(2,1)S(1)} %get-tuple-element.11.refs_2_), channel_id=1, source_target_pairs={{0,16},{16,32},{32,48},{48,64},{64,80},{80,96},{96,112},{112,128},... | collective-permute-start | bytes 786440 | tf_op jit(solution)/shard_map/ppermute | solution.py:269
  113.1 3.8 %collective-permute-done.26.refs_5_ = bf16[512,256]{1,0:T(8,128)(2,1)S(1)} collective-permute-done((bf16[512,256]{1,0:T(8,128)(2,1)S(1)}, bf16[512,256]{1,0:T(8,128)(2,1)S(1)}, u32[]{:S(2)}, u32[]{:S(2)}) %collective-permute-start.26) | collective-permute-done | bytes 262176 | tf_op jit(solution)/shard_map/ppermute | solution.py:269
  116.9 2.8 %collective-permute-done.25.refs_4_ = bf16[512,256]{1,0:T(8,128)(2,1)S(1)} collective-permute-done((bf16[512,256]{1,0:T(8,128)(2,1)S(1)}, bf16[512,256]{1,0:T(8,128)(2,1)S(1)}, u32[]{:S(2)}, u32[]{:S(2)}) %collective-permute-start.25) | collective-permute-done | bytes 262176 | tf_op jit(solution)/shard_map/ppermute | solution.py:269
  119.7 5.1 %shard_map.38 = bf16[1024,256]{1,0:T(8,128)(2,1)} custom-call(s32[1]{0:T(128)} %bitcast.first_ref, bf16[512,256]{1,0:T(8,128)(2,1)S(1)} %get-tuple-element.9.refs_0_, bf16[512,256]{1,0:T(8,128)(2,1)S(1)} %get-tuple-element.10.refs_1_, bf16[512,256]{1,0:T(8,128)(2,1)S(1)} %get-tuple-element.11.refs_2_, bf16[512,256]{1,0:T(8,128)(2,1)S(1)} %get-tuple-element.12.refs_3_, ...), custom_call_target="tpu_custom_call" | custom-call | flops 1342177280 | bytes 2097152 | tf_op jit(solution)/shard_map/pallas_call | solution.py:214
  (48 shorter events, 0.2 us)
Async XLA Ops:
  0.0 8.0 %copy-start.18 = (bf16[336,512]{1,0:T(8,128)(2,1)S(1)}, bf16[336,512]{1,0:T(8,128)(2,1)}, u32[]{:S(2)}) copy-start(bf16[336,512]{1,0:T(8,128)(2,1)} %param.3) | copy-start | bytes 1032196
  0.0 8.0 %collective-permute-start.7 = (bf16[336,512]{1,0:T(8,128)(2,1)}, bf16[336,512]{1,0:T(8,128)(2,1)S(1)}, u32[]{:S(2)}, u32[]{:S(2)}) collective-permute-start(bf16[336,512]{1,0:T(8,128)(2,1)} %param.3), channel_id=1, source_target_pairs={{1,16},{16,1},{3,18},{18,3},{5,20},{20,5},{7,22},{22,7},{9,24},{24... | collective-permute-start | bytes 1032200 | tf_op jit(solution)/shard_map/ppermute | solution.py:54
  1.9 6.1 %copy-start.2 = (bf16[336,512]{1,0:T(8,128)(2,1)}, bf16[336,512]{1,0:T(8,128)(2,1)S(1)}, u32[]{:S(2)}) copy-start(bf16[336,512]{1,0:T(8,128)(2,1)S(1)} %get-tuple-element.15.refs_0_) | copy-start | bytes 1032196
  2.0 6.7 %copy-start = (bf16[336,512]{1,0:T(8,128)(2,1)}, bf16[336,512]{1,0:T(8,128)(2,1)S(1)}, u32[]{:S(2)}) copy-start(bf16[336,512]{1,0:T(8,128)(2,1)S(1)} %get-tuple-element.16.refs_0_) | copy-start | bytes 1032196
  2.0 12.0 %collective-permute-start.17 = (bf16[336,512]{1,0:T(8,128)(2,1)S(1)}, bf16[336,512]{1,0:T(8,128)(2,1)S(1)}, u32[]{:S(2)}, u32[]{:S(2)}) collective-permute-start(bf16[336,512]{1,0:T(8,128)(2,1)S(1)} %get-tuple-element.15.refs_0_), channel_id=1, source_target_pairs={{0,2},{2,4},{4,6},{6,8},{8,10},{10,12},{12,14},{14,0},{1,3},{3,5},... | collective-permute-start | bytes 1032200 | tf_op jit(solution)/shard_map/ppermute | solution.py:31
  4.0 10.0 %collective-permute-start.20 = (bf16[336,512]{1,0:T(8,128)(2,1)S(1)}, bf16[336,512]{1,0:T(8,128)(2,1)S(1)}, u32[]{:S(2)}, u32[]{:S(2)}) collective-permute-start(bf16[336,512]{1,0:T(8,128)(2,1)S(1)} %get-tuple-element.15.refs_0_), channel_id=1, source_target_pairs={{0,14},{2,0},{4,2},{6,4},{8,6},{10,8},{12,10},{14,12},{1,15},{3,1}... | collective-permute-start | bytes 1032200 | tf_op jit(solution)/shard_map/ppermute | solution.py:31
  8.0 9.5 %collective-permute-start.8 = (bf16[336,512]{1,0:T(8,128)(2,1)S(1)}, bf16[336,512]{1,0:T(8,128)(2,1)S(1)}, u32[]{:S(2)}, u32[]{:S(2)}) collective-permute-start(bf16[336,512]{1,0:T(8,128)(2,1)S(1)} %broadcast_select_fusion), channel_id=1, source_target_pairs={{0,128},{128,0},{1,129},{129,1},{2,130},{130,2},{3,131},{131,3},{4... | collective-permute-start | bytes 1032200 | tf_op jit(solution)/shard_map/ppermute | solution.py:35
  8.7 11.8 %collective-permute-start = (bf16[336,512]{1,0:T(8,128)(2,1)S(1)}, bf16[336,512]{1,0:T(8,128)(2,1)S(1)}, u32[]{:S(2)}, u32[]{:S(2)}) collective-permute-start(bf16[336,512]{1,0:T(8,128)(2,1)S(1)} %get-tuple-element.16.refs_0_), channel_id=1, source_target_pairs={{0,2},{2,4},{4,6},{6,8},{8,10},{10,12},{12,14},{14,0},{1,3},{3,5},... | collective-permute-start | bytes 1032200 | tf_op jit(solution)/shard_map/ppermute | solution.py:31
  8.7 15.0 %collective-permute-start.3 = (bf16[336,512]{1,0:T(8,128)(2,1)S(1)}, bf16[336,512]{1,0:T(8,128)(2,1)S(1)}, u32[]{:S(2)}, u32[]{:S(2)}) collective-permute-start(bf16[336,512]{1,0:T(8,128)(2,1)S(1)} %get-tuple-element.16.refs_0_), channel_id=1, source_target_pairs={{0,14},{2,0},{4,2},{6,4},{8,6},{10,8},{12,10},{14,12},{1,15},{3,1}... | collective-permute-start | bytes 1032200 | tf_op jit(solution)/shard_map/ppermute | solution.py:31
  14.0 3.7 %copy-start.5 = (bf16[336,512]{1,0:T(8,128)(2,1)}, bf16[336,512]{1,0:T(8,128)(2,1)S(1)}, u32[]{:S(2)}) copy-start(bf16[336,512]{1,0:T(8,128)(2,1)S(1)} %collective-permute-done.17.refs_1_) | copy-start | bytes 1032196
  14.0 13.6 %collective-permute-start.18 = (bf16[336,512]{1,0:T(8,128)(2,1)S(1)}, bf16[336,512]{1,0:T(8,128)(2,1)}, u32[]{:S(2)}, u32[]{:S(2)}) collective-permute-start(bf16[336,512]{1,0:T(8,128)(2,1)S(1)} %collective-permute-done.17.refs_1_), channel_id=1, source_target_pairs={{0,2},{2,4},{4,6},{6,8},{8,10},{10,12},{12,14},{14,0},{1,3},{3,5},... | collective-permute-start | bytes 1032200 | tf_op jit(solution)/shard_map/ppermute | solution.py:31
  14.0 3.7 %copy-start.8 = (bf16[336,512]{1,0:T(8,128)(2,1)}, bf16[336,512]{1,0:T(8,128)(2,1)S(1)}, u32[]{:S(2)}) copy-start(bf16[336,512]{1,0:T(8,128)(2,1)S(1)} %collective-permute-done.20.refs_2_) | copy-start | bytes 1032196
  14.0 14.3 %collective-permute-start.21 = (bf16[336,512]{1,0:T(8,128)(2,1)S(1)}, bf16[336,512]{1,0:T(8,128)(2,1)S(1)}, u32[]{:S(2)}, u32[]{:S(2)}) collective-permute-start(bf16[336,512]{1,0:T(8,128)(2,1)S(1)} %collective-permute-done.20.refs_2_), channel_id=1, source_target_pairs={{0,14},{2,0},{4,2},{6,4},{8,6},{10,8},{12,10},{14,12},{1,15},{3,1}... | collective-permute-start | bytes 1032200 | tf_op jit(solution)/shard_map/ppermute | solution.py:31
  17.7 23.9 %collective-permute-start.9 = (bf16[2,336,512]{2,1,0:T(8,128)(2,1)S(1)}, bf16[2,336,512]{2,1,0:T(8,128)(2,1)S(1)}, u32[]{:S(2)}, u32[]{:S(2)}) collective-permute-start(bf16[2,336,512]{2,1,0:T(8,128)(2,1)S(1)} %pad_maximum_fusion.refs_5_.refs_3_), channel_id=1, source_target_pairs={{0,32},{32,64},{64,96},{96,0},{1,33},{33,65},{65,97},{97,1},{2,34}... | collective-permute-start | bytes 2064392 | tf_op jit(solution)/shard_map/ppermute | solution.py:31
  20.5 28.7 %collective-permute-start.10 = (bf16[2,336,512]{2,1,0:T(8,128)(2,1)S(1)}, bf16[2,336,512]{2,1,0:T(8,128)(2,1)S(1)}, u32[]{:S(2)}, u32[]{:S(2)}) collective-permute-start(bf16[2,336,512]{2,1,0:T(8,128)(2,1)S(1)} %pad_maximum_fusion.refs_5_.refs_3_), channel_id=1, source_target_pairs={{0,64},{32,96},{64,0},{96,32},{1,65},{33,97},{65,1},{97,33},{2,66}... | collective-permute-start | bytes 2064392 | tf_op jit(solution)/shard_map/ppermute | solution.py:31
  23.7 30.6 %collective-permute-start.11 = (bf16[2,336,512]{2,1,0:T(8,128)(2,1)S(1)}, bf16[2,336,512]{2,1,0:T(8,128)(2,1)S(1)}, u32[]{:S(2)}, u32[]{:S(2)}) collective-permute-start(bf16[2,336,512]{2,1,0:T(8,128)(2,1)S(1)} %pad_maximum_fusion.refs_5_.refs_3_), channel_id=1, source_target_pairs={{0,96},{32,0},{64,32},{96,64},{1,97},{33,1},{65,33},{97,65},{2,98}... | collective-permute-start | bytes 2064392 | tf_op jit(solution)/shard_map/ppermute | solution.py:31
  27.5 9.0 %collective-permute-start.1 = (bf16[336,512]{1,0:T(8,128)(2,1)S(1)}, bf16[336,512]{1,0:T(8,128)(2,1)}, u32[]{:S(2)}, u32[]{:S(2)}) collective-permute-start(bf16[336,512]{1,0:T(8,128)(2,1)S(1)} %collective-permute-done.refs_1_), channel_id=1, source_target_pairs={{0,2},{2,4},{4,6},{6,8},{8,10},{10,12},{12,14},{14,0},{1,3},{3,5},... | collective-permute-start | bytes 1032200 | tf_op jit(solution)/shard_map/ppermute | solution.py:31
  27.5 0.7 copy-start.11
  28.3 10.4 %collective-permute-start.4 = (bf16[336,512]{1,0:T(8,128)(2,1)S(1)}, bf16[336,512]{1,0:T(8,128)(2,1)}, u32[]{:S(2)}, u32[]{:S(2)}) collective-permute-start(bf16[336,512]{1,0:T(8,128)(2,1)S(1)} %collective-permute-done.3.refs_2_), channel_id=1, source_target_pairs={{0,14},{2,0},{4,2},{6,4},{8,6},{10,8},{12,10},{14,12},{1,15},{3,1}... | collective-permute-start | bytes 1032200 | tf_op jit(solution)/shard_map/ppermute | solution.py:31
  31.5 0.7 copy-start.13
  36.5 18.7 %collective-permute-start.22 = (bf16[336,512]{1,0:T(8,128)(2,1)S(1)}, bf16[336,512]{1,0:T(8,128)(2,1)}, u32[]{:S(2)}, u32[]{:S(2)}) collective-permute-start(bf16[336,512]{1,0:T(8,128)(2,1)S(1)} %collective-permute-done.21.refs_4_), channel_id=1, source_target_pairs={{0,14},{2,0},{4,2},{6,4},{8,6},{10,8},{12,10},{14,12},{1,15},{3,1}... | collective-permute-start | bytes 1032200 | tf_op jit(solution)/shard_map/ppermute | solution.py:31
  37.9 0.7 copy-start.15
  38.7 28.1 %collective-permute-start.12 = (bf16[2,336,512]{2,1,0:T(8,128)(2,1)S(1)}, bf16[2,336,512]{2,1,0:T(8,128)(2,1)S(1)}, u32[]{:S(2)}, u32[]{:S(2)}) collective-permute-start(bf16[2,336,512]{2,1,0:T(8,128)(2,1)S(1)} %pad_maximum_fusion.refs_5_.refs_3_), channel_id=1, source_target_pairs={{0,16},{16,0},{1,17},{17,1},{2,18},{18,2},{3,19},{19,3},{4,20},{20... | collective-permute-start | bytes 2064392 | tf_op jit(solution)/shard_map/ppermute | solution.py:35
  41.5 28.5 %collective-permute-start.13 = (bf16[2,336,512]{2,1,0:T(8,128)(2,1)S(1)}, bf16[2,336,512]{2,1,0:T(8,128)(2,1)}, u32[]{:S(2)}, u32[]{:S(2)}) collective-permute-start(bf16[2,336,512]{2,1,0:T(8,128)(2,1)S(1)} %collective-permute-done.9.refs_6_.refs_4_), channel_id=1, source_target_pairs={{0,16},{16,0},{1,17},{17,1},{2,18},{18,2},{3,19},{19,3},{4,20},{20... | collective-permute-start | bytes 2064392 | tf_op jit(solution)/shard_map/ppermute | solution.py:35
  49.2 20.9 %collective-permute-start.14 = (bf16[2,336,512]{2,1,0:T(8,128)(2,1)S(1)}, bf16[2,336,512]{2,1,0:T(8,128)(2,1)}, u32[]{:S(2)}, u32[]{:S(2)}) collective-permute-start(bf16[2,336,512]{2,1,0:T(8,128)(2,1)S(1)} %collective-permute-done.10.refs_7_.refs_5_), channel_id=1, source_target_pairs={{0,16},{16,0},{1,17},{17,1},{2,18},{18,2},{3,19},{19,3},{4,20},{20... | collective-permute-start | bytes 2064392 | tf_op jit(solution)/shard_map/ppermute | solution.py:35
  54.3 17.9 %collective-permute-start.15 = (bf16[2,336,512]{2,1,0:T(8,128)(2,1)S(1)}, bf16[2,336,512]{2,1,0:T(8,128)(2,1)}, u32[]{:S(2)}, u32[]{:S(2)}) collective-permute-start(bf16[2,336,512]{2,1,0:T(8,128)(2,1)S(1)} %collective-permute-done.11.refs_8_.refs_6_), channel_id=1, source_target_pairs={{0,16},{16,0},{1,17},{17,1},{2,18},{18,2},{3,19},{19,3},{4,20},{20... | collective-permute-start | bytes 2064392 | tf_op jit(solution)/shard_map/ppermute | solution.py:35
  55.3 11.5 %collective-permute-start.2 = (bf16[336,512]{1,0:T(8,128)(2,1)}, bf16[336,512]{1,0:T(8,128)(2,1)}, u32[]{:S(2)}, u32[]{:S(2)}) collective-permute-start(bf16[336,512]{1,0:T(8,128)(2,1)} %collective-permute-done.1.refs_3_), channel_id=1, source_target_pairs={{0,2},{2,4},{4,6},{6,8},{8,10},{10,12},{12,14},{14,0},{1,3},{3,5},... | collective-permute-start | bytes 1032200 | tf_op jit(solution)/shard_map/ppermute | solution.py:31
  66.8 13.1 %collective-permute-start.19 = (bf16[336,512]{1,0:T(8,128)(2,1)}, bf16[336,512]{1,0:T(8,128)(2,1)}, u32[]{:S(2)}, u32[]{:S(2)}) collective-permute-start(bf16[336,512]{1,0:T(8,128)(2,1)} %collective-permute-done.18.refs_3_), channel_id=1, source_target_pairs={{0,2},{2,4},{4,6},{6,8},{8,10},{10,12},{12,14},{14,0},{1,3},{3,5},... | collective-permute-start | bytes 1032200 | tf_op jit(solution)/shard_map/ppermute | solution.py:31
  66.8 13.1 %collective-permute-start.23 = (bf16[336,512]{1,0:T(8,128)(2,1)}, bf16[336,512]{1,0:T(8,128)(2,1)}, u32[]{:S(2)}, u32[]{:S(2)}) collective-permute-start(bf16[336,512]{1,0:T(8,128)(2,1)} %collective-permute-done.22.refs_1_), channel_id=1, source_target_pairs={{0,14},{2,0},{4,2},{6,4},{8,6},{10,8},{12,10},{14,12},{1,15},{3,1}... | collective-permute-start | bytes 1032200 | tf_op jit(solution)/shard_map/ppermute | solution.py:31
  70.1 16.3 %collective-permute-start.5 = (bf16[336,512]{1,0:T(8,128)(2,1)}, bf16[336,512]{1,0:T(8,128)(2,1)}, u32[]{:S(2)}, u32[]{:S(2)}) collective-permute-start(bf16[336,512]{1,0:T(8,128)(2,1)} %collective-permute-done.4.refs_4_), channel_id=1, source_target_pairs={{0,14},{2,0},{4,2},{6,4},{8,6},{10,8},{12,10},{14,12},{1,15},{3,1}... | collective-permute-start | bytes 1032200 | tf_op jit(solution)/shard_map/ppermute | solution.py:31
  70.1 16.3 %collective-permute-start.6 = (bf16[336,512]{1,0:T(8,128)(2,1)}, bf16[336,512]{1,0:T(8,128)(2,1)}, u32[]{:S(2)}, u32[]{:S(2)}) collective-permute-start(bf16[336,512]{1,0:T(8,128)(2,1)} %collective-permute-done.2.refs_0_), channel_id=1, source_target_pairs={{0,2},{2,4},{4,6},{6,8},{8,10},{10,12},{12,14},{14,0},{1,3},{3,5},... | collective-permute-start | bytes 1032200 | tf_op jit(solution)/shard_map/ppermute | solution.py:31
  72.2 1.0 copy-start.3
  73.1 1.0 copy-start.6
  74.1 1.0 copy-start.9
  75.1 1.0 copy-start.16
  79.8 2.9 %copy-start.1 = (bf16[336,512]{1,0:T(8,128)(2,1)S(1)}, bf16[336,512]{1,0:T(8,128)(2,1)}, u32[]{:S(2)}) copy-start(bf16[336,512]{1,0:T(8,128)(2,1)} %copy-done) | copy-start | bytes 1032196
  79.8 2.9 %copy-start.12 = (bf16[336,512]{1,0:T(8,128)(2,1)S(1)}, bf16[336,512]{1,0:T(8,128)(2,1)}, u32[]{:S(2)}) copy-start(bf16[336,512]{1,0:T(8,128)(2,1)} %copy-done.11) | copy-start | bytes 1032196
  79.8 2.9 %copy-start.14 = (bf16[336,512]{1,0:T(8,128)(2,1)S(1)}, bf16[336,512]{1,0:T(8,128)(2,1)}, u32[]{:S(2)}) copy-start(bf16[336,512]{1,0:T(8,128)(2,1)} %copy-done.13) | copy-start | bytes 1032196
  82.6 24.2 %collective-permute-start.24 = (bf16[512,512]{1,0:T(8,128)(2,1)S(1)}, bf16[512,512]{1,0:T(8,128)(2,1)S(1)}, u32[]{:S(2)}, u32[]{:S(2)}) collective-permute-start(bf16[512,512]{1,0:T(8,128)(2,1)S(1)} %shard_map.36), channel_id=1, source_target_pairs={{0,1},{1,0},{2,3},{3,2},{4,5},{5,4},{6,7},{7,6},{8,9},{9,8},{10,11... | collective-permute-start | bytes 1572872 | tf_op jit(solution)/shard_map/ppermute | solution.py:35
  89.2 19.9 %collective-permute-start.16 = (bf16[512,512]{1,0:T(8,128)(2,1)S(1)}, bf16[512,512]{1,0:T(8,128)(2,1)S(1)}, u32[]{:S(2)}, u32[]{:S(2)}) collective-permute-start(bf16[512,512]{1,0:T(8,128)(2,1)S(1)} %shard_map.31), channel_id=1, source_target_pairs={{0,1},{1,0},{2,3},{3,2},{4,5},{5,4},{6,7},{7,6},{8,9},{9,8},{10,11... | collective-permute-start | bytes 1572872 | tf_op jit(solution)/shard_map/ppermute | solution.py:35
  94.0 1.0 copy-start.4
  94.0 1.1 copy-start.7
  94.0 1.2 copy-start.10
  94.0 1.3 %copy-start.17 = (bf16[336,512]{1,0:T(8,128)(2,1)S(1)}, bf16[336,512]{1,0:T(8,128)(2,1)}, u32[]{:S(2)}) copy-start(bf16[336,512]{1,0:T(8,128)(2,1)} %copy-done.15) | copy-start | bytes 1032196
  107.1 9.8 %collective-permute-start.26 = (bf16[512,256]{1,0:T(8,128)(2,1)S(1)}, bf16[512,256]{1,0:T(8,128)(2,1)S(1)}, u32[]{:S(2)}, u32[]{:S(2)}) collective-permute-start(bf16[512,256]{1,0:T(8,128)(2,1)S(1)} %get-tuple-element.12.refs_3_), channel_id=1, source_target_pairs={{0,16},{16,32},{32,48},{48,64},{64,80},{80,96},{96,112},{112,128},... | collective-permute-start | bytes 786440 | tf_op jit(solution)/shard_map/ppermute | solution.py:269
  109.4 10.3 %collective-permute-start.25 = (bf16[512,256]{1,0:T(8,128)(2,1)S(1)}, bf16[512,256]{1,0:T(8,128)(2,1)S(1)}, u32[]{:S(2)}, u32[]{:S(2)}) collective-permute-start(bf16[512,256]{1,0:T(8,128)(2,1)S(1)} %get-tuple-element.11.refs_2_), channel_id=1, source_target_pairs={{0,16},{16,32},{32,48},{48,64},{64,80},{80,96},{96,112},{112,128},... | collective-permute-start | bytes 786440 | tf_op jit(solution)/shard_map/ppermute | solution.py:269

commit v2 on v1

v2 whole, which is shorter than its diff:
```python
import functools

import jax
import jax.numpy as jnp
from jax import lax
from jax.experimental import pallas as pl
from jax.experimental.pallas import tpu as pltpu
from jax.sharding import Mesh
from jax.sharding import PartitionSpec as P

HEAD = 128
Q_PER_KV = 2
WINDOW = 1024
ROPE_BASE = 10000.0
SCALE = 168.0 ** (-0.5)
LOG2E = 1.4426950408889634
MASKED = -1e30

AXES = ("x_lo", "y", "core", "z", "x_hi")
SIZES = (2, 4, 2, 8, 2)
CTX = ("x_lo", "y", "core")
HEADS = ("z", "x_hi")

TILE = 256
DISTANCES = (0, -1, 1, -2, 2, -3, 3, 4)
VMEM_BYTES = 12 * 1024 * 1024


def hop(block, axis, distance):
    n = lax.axis_size(axis)
    return lax.ppermute(block, axis, [(i, (i + distance) % n) for i in range(n)])


def swap(block, axis):
    return lax.ppermute(block, axis, [(0, 1), (1, 0)])


def after(value, *others):
    return lax.optimization_barrier((value, *others))[0]


def gather(tokens, w, where, tables):
    core, x_hi = lax.axis_index("core"), lax.axis_index("x_hi")
    tie = lax.optimization_barrier
    high, low = tokens

    def step(pair):
        return hop(pair[0], "z", 1), hop(pair[1], "z", -1)

    high_1 = step((high, high))
    low_1 = step((low, low))
    crossed = lax.ppermute(w, ("core", "x_hi"), [(1, 2), (2, 1)])
    route = [
        ((l * 2 + c) * 2 + a, ((1 - l) * 2 + a) * 2 + c)
        for l in range(2)
        for c in range(2)
        for a in range(2)
    ]
    other = lax.ppermute(w, ("x_lo", "core", "x_hi"), route)
    pair = jnp.stack([jnp.where(core == x_hi, w, crossed), other])

    high_1, pair, tables = tie((high_1, pair, tables))
    high_2 = step(high_1)
    w_ahead, w_behind = hop(pair, "y", 1), hop(pair, "y", -1)
    pair_swapped = swap(pair, "core")

    high_2, low_1 = tie((high_2, low_1))
    high_3 = step(high_2)
    low_2 = step(low_1)

    low_2, w_ahead, w_behind = tie((low_2, w_ahead, w_behind))
    low_3 = step(low_2)
    route = [(i * 2 + c, (i + 1 - 2 * c) % 4 * 2 + c) for i in range(4) for c in range(2)]
    opposite = lax.ppermute(jnp.where(core == 0, w_ahead, w_behind), ("y", "core"), route)
    ahead_swapped, behind_swapped = swap(w_ahead, "core"), swap(w_behind, "core")

    high_3, low_2 = tie((high_3, low_2))
    high_4 = hop(high_3[0], "z", 1)
    blocks = [pair, w_ahead, opposite, w_behind]
    blocks += [pair_swapped, ahead_swapped, swap(opposite, "core"), behind_swapped]
    weights = collect(where, blocks)

    low_4 = hop(low_3[1], "z", -1)

    shards = [
        [high, *high_1, *high_2, *high_3, high_4],
        [low, *low_1, *low_2, *low_3, low_4],
    ]
    return shards, weights, tables


def collect_kernel(where_ref, *refs):
    blocks, out_ref, sems = refs[:8], refs[8], refs[9]
    y_rel, x_rel, keep = where_ref[0], where_ref[1], where_ref[2]
    n = blocks[0].shape[-1]
    for half in range(2):
        columns = pl.ds(pl.multiple_of((half ^ keep) * n, n), n)
        for x in range(2):
            for k in range(4):
                place = (x ^ x_rel) * 4 + ((y_rel - k) & 3)
                pltpu.make_async_copy(
                    blocks[half * 4 + k].at[x],
                    out_ref.at[place, :, columns],
                    sems.at[(half * 2 + x) * 4 + k],
                ).start()
    for half in range(2):
        for x in range(2):
            for k in range(4):
                pltpu.make_async_copy(
                    blocks[half * 4 + k].at[x],
                    out_ref.at[0, :, pl.ds(0, n)],
                    sems.at[(half * 2 + x) * 4 + k],
                ).wait()


def collect(where, blocks):
    _, k, n = blocks[0].shape
    anywhere = pl.BlockSpec(memory_space=pl.ANY)
    return pl.pallas_call(
        collect_kernel,
        out_shape=jax.ShapeDtypeStruct((8, k, 2 * n), jnp.bfloat16),
        in_specs=[pl.BlockSpec(memory_space=pltpu.SMEM)] + [anywhere] * 8,
        out_specs=pl.BlockSpec(memory_space=pltpu.VMEM),
        scratch_shapes=[pltpu.SemaphoreType.DMA((16,))],
        compiler_params=pltpu.CompilerParams(vmem_limit_bytes=VMEM_BYTES),
        cost_estimate=pl.CostEstimate(flops=0, bytes_accessed=4 * 8 * k * n, transcendentals=0),
    )(where, *blocks)


def product_kernel(half, z_ref, weights_ref, *refs):
    tokens, out_ref = refs[:-1], refs[-1]
    z = z_ref[0]
    width = weights_ref.shape[-1] // 2
    lhs = jnp.concatenate([t[...] for t in tokens], axis=0)
    rhs = jnp.concatenate(
        [weights_ref[(z + d + 8) & 7, :, pl.ds(half * width, width)] for d in DISTANCES], axis=0
    )
    total = lax.dot_general(
        lhs, rhs, (((0,), (0,)), ((), ())), preferred_element_type=jnp.float32
    )
    out_ref[...] = total.astype(out_ref.dtype)


def product(z, shards, weights, half, dtype):
    depth, rows = shards[0].shape
    width = weights.shape[-1] // 2
    vmem = pl.BlockSpec(memory_space=pltpu.VMEM)
    return pl.pallas_call(
        functools.partial(product_kernel, half),
        out_shape=jax.ShapeDtypeStruct((rows, width), dtype),
        in_specs=[pl.BlockSpec(memory_space=pltpu.SMEM)] + [vmem] * 9,
        out_specs=vmem,
        compiler_params=pltpu.CompilerParams(vmem_limit_bytes=VMEM_BYTES),
        cost_estimate=pl.CostEstimate(
            flops=2 * 8 * depth * rows * width,
            bytes_accessed=2 * 8 * depth * (rows + width),
            transcendentals=0,
        ),
    )(z, weights, *shards)


def finish_kernel(keep_ref, sent_ref, cos_ref, sin_ref, q_ref, kv_ref):
    cos, sin = cos_ref[...], sin_ref[...]
    for j in range(4):
        columns = pl.ds(j * HEAD, HEAD)
        block = keep_ref[:, columns] + sent_ref[:, columns].astype(jnp.float32)
        if j < 3:
            block = block * cos + pltpu.roll(block, HEAD // 2, 1) * sin
        block = block.astype(jnp.bfloat16)
        if j < 2:
            q_ref[:, columns] = block
        else:
            kv_ref[:, pl.ds((j - 2) * HEAD, HEAD)] = block


def finish(keep, sent, cos, sin):
    rows = keep.shape[0]
    vmem = pl.BlockSpec(memory_space=pltpu.VMEM)
    return pl.pallas_call(
        finish_kernel,
        out_shape=[jax.ShapeDtypeStruct((rows, 2 * HEAD), jnp.bfloat16)] * 2,
        in_specs=[vmem] * 4,
        out_specs=[vmem] * 2,
        compiler_params=pltpu.CompilerParams(vmem_limit_bytes=VMEM_BYTES),
        cost_estimate=pl.CostEstimate(
            flops=rows * 2048, bytes_accessed=rows * 6000, transcendentals=0
        ),
    )(keep, sent, cos, sin)


def attend_kernel(plan, n_keys, has_state, last, joins, first_ref, q_ref, *refs):
    keys, refs = refs[:n_keys], refs[n_keys:]
    state, refs = (refs[:3], refs[3:]) if has_state else (None, refs)
    if joins:
        below_ref, refs = refs[0], refs[1:]
        refs[0][pl.ds(len(plan) * TILE, below_ref.shape[0]), :] = below_ref[...]
    outside = jnp.where(first_ref[0] == 0, jnp.float32(MASKED), jnp.float32(0))
    row = lax.broadcasted_iota(jnp.int32, (2 * TILE, TILE), 0) % TILE
    column = lax.broadcasted_iota(jnp.int32, (2 * TILE, TILE), 1)
    later = column > row
    factor = SCALE * LOG2E
    for i, tiles in enumerate(plan):
        rows = pl.ds(i * TILE, TILE)
        both = pl.ds(i * 2 * TILE, 2 * TILE)
        q = jnp.concatenate([q_ref[rows, :HEAD], q_ref[rows, HEAD:]], axis=0)
        scores = []
        for source, tile, before, masked in tiles:
            s = lax.dot_general(
                q,
                keys[source][pl.ds(tile * TILE, TILE), :HEAD],
                (((1,), (1,)), ((), ())),
                preferred_element_type=jnp.float32,
            )
            if before:
                s = s + outside
            if masked:
                s = jnp.where(later, s, MASKED) if before else jnp.where(later, MASKED, s)
            scores.append(s)
        highest = jnp.max(functools.reduce(jnp.maximum, scores), axis=-1, keepdims=True)
        highest = jnp.broadcast_to(highest, (2 * TILE, HEAD))
        if has_state:
            highest = jnp.maximum(highest, state[0][both, :])
        shift = highest * factor
        wide = jnp.concatenate([shift] * (TILE // HEAD), axis=1)
        total, summed = None, None
        for s, (source, tile, _, _) in zip(scores, tiles):
            p = jnp.exp2(s * factor - wide)
            total = p if total is None else total + p
            part = jnp.dot(
                p.astype(jnp.bfloat16),
                keys[source][pl.ds(tile * TILE, TILE), HEAD:],
                preferred_element_type=jnp.float32,
            )
            summed = part if summed is None else summed + part
        total = jnp.broadcast_to(jnp.sum(total, axis=-1, keepdims=True), (2 * TILE, HEAD))
        if has_state:
            shrink = jnp.exp2(state[0][both, :] * factor - shift)
            total = total + state[1][both, :] * shrink
            summed = summed + state[2][both, :] * shrink
        if last:
            out = (summed / total).astype(jnp.bfloat16)
            refs[0][rows, :HEAD] = out[:TILE]
            refs[0][rows, HEAD:] = out[TILE:]
        else:
            refs[0][both, :] = highest
            refs[1][both, :] = total
            refs[2][both, :] = summed


def attend(first, queries, keys, plan, state, last, below=None):
    rows = queries.shape[0]
    vmem = pl.BlockSpec(memory_space=pltpu.VMEM)
    operands = [first, queries, *keys] + ([] if state is None else list(state))
    if below is not None:
        operands.append(below)
    if last:
        joined = rows + (0 if below is None else below.shape[0])
        shapes = [jax.ShapeDtypeStruct((joined, 2 * HEAD), jnp.bfloat16)]
    else:
        shapes = [jax.ShapeDtypeStruct((2 * rows, HEAD), jnp.float32)] * 3
    pairs = sum(len(tiles) for tiles in plan) * 2 * TILE * TILE
    result = pl.pallas_call(
        functools.partial(
            attend_kernel, plan, len(keys), state is not None, last, below is not None
        ),
        out_shape=shapes,
        in_specs=[pl.BlockSpec(memory_space=pltpu.SMEM)] + [vmem] * (len(operands) - 1),
        out_specs=[vmem] * len(shapes),
        compiler_params=pltpu.CompilerParams(vmem_limit_bytes=VMEM_BYTES),
        cost_estimate=pl.CostEstimate(
            flops=4 * pairs * HEAD, bytes_accessed=rows * 4096, transcendentals=pairs
        ),
    )(*operands)
    return result[0] if last else result


def rotary_tables(positions):
    half = HEAD // 2
    inverse = jnp.power(ROPE_BASE, -2.0 * jnp.arange(half, dtype=jnp.float32) / HEAD)
    angles = positions.astype(jnp.float32)[:, None] * inverse[None, :]
    cos, sin = jnp.cos(angles), jnp.sin(angles)
    return jnp.concatenate([cos, cos], axis=1), jnp.concatenate([-sin, sin], axis=1)


def on_device(tokens, w_qkv):
    row_count = tokens.shape[0]
    rows = row_count // 2
    x_lo, y, core, z, x_hi = (lax.axis_index(a) for a in AXES)
    ctx = (x_lo * 4 + y) * 2 + core
    positions = ctx * row_count + jnp.arange(row_count, dtype=jnp.int32)
    cos, sin = rotary_tables(positions)

    z_place = z.astype(jnp.int32)[None]
    where = jnp.stack([y, x_lo, jnp.where(core == x_hi, 0, 1)]).astype(jnp.int32)

    spans = (slice(rows, row_count), slice(0, rows))
    shards, weights, (cos, sin) = gather(
        [tokens[span].T for span in spans], w_qkv, where, (cos, sin)
    )

    tie = lax.optimization_barrier
    send_high = product(z_place, shards[0], weights, 1, jnp.bfloat16)
    sent_high = swap(send_high, "x_hi")
    send_high, z_place = tie((send_high, z_place))
    send_low = product(z_place, shards[1], weights, 1, jnp.bfloat16)
    sent_low = swap(send_low, "x_hi")
    send_low, z_place = tie((send_low, z_place))
    keep_high, keep_low = (product(z_place, s, weights, 0, jnp.float32) for s in shards)
    sent_high, keep_high, keep_low = tie((sent_high, keep_high, keep_low))
    q_high, own_high = finish(keep_high, sent_high, cos[rows:], sin[rows:])
    before_high = lax.ppermute(own_high, CTX, [(c, c + 1) for c in range(15)])
    q_low, own_low = finish(keep_low, sent_low, cos[:rows], sin[:rows])
    before_low = lax.ppermute(own_low, CTX, [(c, c + 1) for c in range(15)])

    first = ctx.astype(jnp.int32)[None]
    high = attend(
        first,
        q_high,
        [before_high, own_high],
        (
            ((0, 0, True, True), (0, 1, True, False), (1, 0, False, True)),
            ((0, 1, True, True), (1, 0, False, False), (1, 1, False, True)),
        ),
        None,
        False,
    )
    high = attend(
        first, q_high, [own_low], (((0, 0, False, False), (0, 1, False, False)),) * 2, high, True
    )
    low = attend(
        first,
        q_low,
        [before_high, own_low],
        (
            ((0, 0, True, False), (0, 1, True, False), (1, 0, False, True)),
            ((0, 0, True, False), (0, 1, True, False), (1, 0, False, False), (1, 1, False, True)),
        ),
        None,
        False,
    )
    return attend(
        first,
        q_low,
        [before_low],
        (((0, 0, True, True), (0, 1, True, False)), ((0, 1, True, True),)),
        low,
        True,
        high,
    )


def solution(mesh):
    fine = Mesh(mesh.devices.reshape(SIZES), AXES)
    placed = P(CTX, HEADS)
    return jax.shard_map(
        on_device, mesh=fine, in_specs=(placed, placed), out_specs=placed, check_vma=False
    )
```

time: 127 us -> 115 us (0.906); the launches traced: 125 us -> 115 us
  Pallas kernels: 30 us -> 21.3 us
  waiting for transfers between devices: 37.2 us -> 42.7 us
  local copies, waits for them, and re-layouts: 8.21 us -> 3.75 us
  starting transfers between devices: 46.6 us -> 43.5 us
    ppermute x7 -> x6, waiting for transfers between devices: 0.02 us -> 10.1 us  [swap(): return lax.ppermute(block, axis, [(0, 1), (1, 0)])]
    pallas_call x9, Pallas kernels: 29.4 us -> 20.6 us  [the longest x4 11.6 us: product(): pl.pallas_call(functools.partial(product_kernel, half), out_shape=jax.Sha...]
    unnamed x38 -> x16, local copies, waits for them, and re-layouts: 7.08 us -> 1.47 us
    ppermute x7 -> x6, starting transfers between devices: 11.5 us -> 6.83 us  [swap(): return lax.ppermute(block, axis, [(0, 1), (1, 0)])]
    ppermute x3 -> x5, waiting for transfers between devices: 6.61 us -> 3.62 us  [the longest x1 3.18 us: on_device(): before_low = lax.ppermute(own_low, CTX, [(c, c + 1) for c in range(15)])]
    ppermute x17 -> x16, starting transfers between devices: 28.6 us -> 30.8 us  [hop(): lax.ppermute(block, axis, [(i, (i + distance) % n) for i in range(n)])]
    neg x0 -> x1, other arithmetic: none -> 1.9 us  [rotary_tables(): -sin]
    sin x1 -> x0, other arithmetic: 1.9 us -> none  [rotary_tables(): cos, sin = (jnp.cos(angles), jnp.sin(angles))]
  transfers between devices with their start and end apart: 27 -> 27, of which waited for: 9 -> 12; matrix products, arithmetic and copies ran while one was open for 3% -> 4% of each run, Pallas kernels for 20% -> 17%
where the time goes in v2:
time: 115 us
  starting transfers between devices  43.5 us (38%)
  waiting for transfers between devices  42.7 us (37%)
  Pallas kernels  21.3 us (19%)
  local copies, waits for them, and re-layouts  3.75 us (3%)
  other arithmetic  3.47 us (3%)
    ppermute x16, starting transfers between devices, hop(): lax.ppermute(block, axis, [(i, (i + distance) % n) for i in range(n)])  30.8 us
    ppermute x16, waiting for transfers between devices, hop(): lax.ppermute(block, axis, [(i, (i + distance) % n) for i in range(n)])  28.9 us
    pallas_call x4, Pallas kernels, product(): pl.pallas_call(functools.partial(product_kernel, half), out_shape=jax.Sha...  11.6 us
    ppermute x6, waiting for transfers between devices, swap(): return lax.ppermute(block, axis, [(0, 1), (1, 0)])  10.1 us
    ppermute x6, starting transfers between devices, swap(): return lax.ppermute(block, axis, [(0, 1), (1, 0)])  6.83 us
    pallas_call x4, Pallas kernels, attend(): pl.pallas_call(functools.partial(attend_kernel, plan, len(keys), state is...  6.39 us
    ppermute x1, waiting for transfers between devices, on_device(): before_low = lax.ppermute(own_low, CTX, [(c, c + 1) for c in range(15)])  3.18 us
    pallas_call x1, Pallas kernels, collect(): pl.pallas_call(collect_kernel, out_shape=jax.ShapeDtypeStruct((8, k, 2 *...  2.68 us
  transfers between devices with their start and end apart: 27, of which 12 were waited for; matrix products, arithmetic and copies ran while one was open for 4% of the time, Pallas kernels for 17%

profile of v2, /device:TPU:2, one launch (start us, length us, event | category | flops | bytes accessed | tf_op | source)
XLA Modules:
  0.0 114.9 jit_solution(8384403223922241984)
XLA Ops:
  0.0 1.2 %slice_bitcast_fusion = (bf16[336,512]{1,0:T(8,128)(2,1)S(1)}, bf16[336,512]{1,0:T(8,128)(2,1)S(1)}) fusion(bf16[1024,336]{0,1:T(8,128)(2,1)} %param.2), kind=kLoop, calls=%fused_computation.6 | loop fusion | bytes 1376256 | tf_op jit(solution)/shard_map/transpose | solution.py:298
  1.2 2.0 %collective-permute-start = (bf16[336,512]{1,0:T(8,128)(2,1)S(1)}, bf16[336,512]{1,0:T(8,128)(2,1)S(1)}, u32[]{:S(2)}, u32[]{:S(2)}) collective-permute-start(bf16[336,512]{1,0:T(8,128)(2,1)S(1)} %get-tuple-element.70.refs_0_), channel_id=1, source_target_pairs={{0,2},{2,4},{4,6},{6,8},{8,10},{10,12},{12,14},{14,0},{1,3},{3,5},... | collective-permute-start | bytes 1032200 | tf_op jit(solution)/shard_map/ppermute | solution.py:31
  3.2 4.0 %collective-permute-start.1 = (bf16[336,512]{1,0:T(8,128)(2,1)S(1)}, bf16[336,512]{1,0:T(8,128)(2,1)S(1)}, u32[]{:S(2)}, u32[]{:S(2)}) collective-permute-start(bf16[336,512]{1,0:T(8,128)(2,1)S(1)} %get-tuple-element.70.refs_0_), channel_id=1, source_target_pairs={{0,14},{2,0},{4,2},{6,4},{8,6},{10,8},{12,10},{14,12},{1,15},{3,1}... | collective-permute-start | bytes 1032200 | tf_op jit(solution)/shard_map/ppermute | solution.py:31
  7.2 0.5 collective-permute-start.3
  7.7 0.7 collective-permute-start.2
  8.4 0.1 collective-permute-start.6
  8.6 1.9 %fusion = (f32[1024,64]{1,0:T(8,128)S(1)}, f32[1024,64]{1,0:T(8,128)S(1)}, f32[1024,64]{1,0:T(8,128)S(1)}) fusion(f32[64]{0:T(128)S(1)} %multiply_power_fusion, f32[1024]{0:T(1024)S(1)} %add_convert_fusion), kind=kLoop, calls=%fused_computation.9 | loop fusion | flops 131072 | bytes 790784 | tf_op jit(solution)/shard_map/neg | solution.py:282
  10.5 1.3 %pad_maximum_fusion.1 = (f32[1024,128]{1,0:T(8,128)}, f32[1024,128]{1,0:T(8,128)}) fusion(f32[1024,64]{1,0:T(8,128)S(1)} %get-tuple-element.77, f32[1024,64]{1,0:T(8,128)S(1)} %get-tuple-element.76, f32[1024,64]{1,0:T(8,128)S(1)} %get-tuple-element.75), kind=kLoop, calls=%fused_computation.4 | loop fusion | flops 262144 | bytes 1835008 | tf_op jit(solution)/shard_map/concatenate | solution.py:282
  11.8 3.2 %collective-permute-start.7 = (bf16[336,512]{1,0:T(8,128)(2,1)S(1)}, bf16[336,512]{1,0:T(8,128)(2,1)}, u32[]{:S(2)}, u32[]{:S(2)}) collective-permute-start(bf16[336,512]{1,0:T(8,128)(2,1)S(1)} %get-tuple-element.69.refs_0_), channel_id=1, source_target_pairs={{0,14},{2,0},{4,2},{6,4},{8,6},{10,8},{12,10},{14,12},{1,15},{3,1}... | collective-permute-start | bytes 1032200 | tf_op jit(solution)/shard_map/ppermute | solution.py:31
  15.0 0.4 collective-permute-done.3
  15.4 0.1 pad_maximum_fusion.refs_0_
  15.5 0.0 collective-permute-done.refs_1_
  15.5 0.0 collective-permute-done.1.refs_2_
  15.5 0.1 collective-permute-start.4
  15.6 3.2 %collective-permute-start.5 = (bf16[336,512]{1,0:T(8,128)(2,1)S(1)}, bf16[336,512]{1,0:T(8,128)(2,1)S(1)}, u32[]{:S(2)}, u32[]{:S(2)}) collective-permute-start(bf16[336,512]{1,0:T(8,128)(2,1)S(1)} %collective-permute-done.1.refs_2_), channel_id=1, source_target_pairs={{0,14},{2,0},{4,2},{6,4},{8,6},{10,8},{12,10},{14,12},{1,15},{3,1}... | collective-permute-start | bytes 1032200 | tf_op jit(solution)/shard_map/ppermute | solution.py:31
  18.8 1.6 %collective-permute-start.10 = (bf16[2,336,512]{2,1,0:T(8,128)(2,1)S(1)}, bf16[2,336,512]{2,1,0:T(8,128)(2,1)S(1)}, u32[]{:S(2)}, u32[]{:S(2)}) collective-permute-start(bf16[2,336,512]{2,1,0:T(8,128)(2,1)S(1)} %pad_maximum_fusion.refs_0_), channel_id=1, source_target_pairs={{0,32},{32,64},{64,96},{96,0},{1,33},{33,65},{65,97},{97,1},{2,34}... | collective-permute-start | bytes 2064392 | tf_op jit(solution)/shard_map/ppermute | solution.py:31
  20.4 2.1 %collective-permute-done.6.refs_1_ = bf16[336,512]{1,0:T(8,128)(2,1)} collective-permute-done((bf16[336,512]{1,0:T(8,128)(2,1)S(1)}, bf16[336,512]{1,0:T(8,128)(2,1)}, u32[]{:S(2)}, u32[]{:S(2)}) %collective-permute-start.6) | collective-permute-done | bytes 344096 | tf_op jit(solution)/shard_map/ppermute | solution.py:31
  22.5 3.0 %collective-permute-start.11 = (bf16[2,336,512]{2,1,0:T(8,128)(2,1)S(1)}, bf16[2,336,512]{2,1,0:T(8,128)(2,1)S(1)}, u32[]{:S(2)}, u32[]{:S(2)}) collective-permute-start(bf16[2,336,512]{2,1,0:T(8,128)(2,1)S(1)} %pad_maximum_fusion.refs_0_), channel_id=1, source_target_pairs={{0,96},{32,0},{64,32},{96,64},{1,97},{33,1},{65,33},{97,65},{2,98}... | collective-permute-start | bytes 2064392 | tf_op jit(solution)/shard_map/ppermute | solution.py:31
  25.5 0.0 collective-permute-done.7.refs_2_
  25.5 1.7 %collective-permute-done.4.refs_3_ = bf16[336,512]{1,0:T(8,128)(2,1)S(1)} collective-permute-done((bf16[336,512]{1,0:T(8,128)(2,1)S(1)}, bf16[336,512]{1,0:T(8,128)(2,1)S(1)}, u32[]{:S(2)}, u32[]{:S(2)}) %collective-permute-start.4) | collective-permute-done | bytes 344096 | tf_op jit(solution)/shard_map/ppermute | solution.py:31
  27.2 0.0 collective-permute-done.5.refs_4_
  27.2 0.7 copy-done
  28.0 1.9 %collective-permute-start.8 = (bf16[336,512]{1,0:T(8,128)(2,1)}, bf16[336,512]{1,0:T(8,128)(2,1)}, u32[]{:S(2)}, u32[]{:S(2)}) collective-permute-start(bf16[336,512]{1,0:T(8,128)(2,1)} %collective-permute-done.6.refs_1_), channel_id=1, source_target_pairs={{0,2},{2,4},{4,6},{6,8},{8,10},{10,12},{12,14},{14,0},{1,3},{3,5},... | collective-permute-start | bytes 1032200 | tf_op jit(solution)/shard_map/ppermute | solution.py:31
  29.9 2.9 %collective-permute-start.9 = (bf16[336,512]{1,0:T(8,128)(2,1)}, bf16[336,512]{1,0:T(8,128)(2,1)}, u32[]{:S(2)}, u32[]{:S(2)}) collective-permute-start(bf16[336,512]{1,0:T(8,128)(2,1)} %collective-permute-done.7.refs_2_), channel_id=1, source_target_pairs={{0,14},{2,0},{4,2},{6,4},{8,6},{10,8},{12,10},{14,12},{1,15},{3,1}... | collective-permute-start | bytes 1032200 | tf_op jit(solution)/shard_map/ppermute | solution.py:31
  32.8 6.4 %collective-permute-done.8.refs_3_ = bf16[336,512]{1,0:T(8,128)(2,1)} collective-permute-done((bf16[336,512]{1,0:T(8,128)(2,1)}, bf16[336,512]{1,0:T(8,128)(2,1)}, u32[]{:S(2)}, u32[]{:S(2)}) %collective-permute-start.8) | collective-permute-done | bytes 344096 | tf_op jit(solution)/shard_map/ppermute | solution.py:31
  39.1 0.5 collective-permute-done.9.refs_4_
  39.7 0.0 collective-permute-done.10.refs_1_
  39.7 1.2 %collective-permute-done.11.refs_3_ = bf16[2,336,512]{2,1,0:T(8,128)(2,1)S(1)} collective-permute-done((bf16[2,336,512]{2,1,0:T(8,128)(2,1)S(1)}, bf16[2,336,512]{2,1,0:T(8,128)(2,1)S(1)}, u32[]{:S(2)}, u32[]{:S(2)}) %collective-permute-start.11) | collective-permute-done | bytes 688160 | tf_op jit(solution)/shard_map/ppermute | solution.py:31
  40.9 0.1 broadcast_select_fusion
  40.9 0.8 collective-permute-start.12
  41.7 3.0 %collective-permute-start.13 = (bf16[2,336,512]{2,1,0:T(8,128)(2,1)S(1)}, bf16[2,336,512]{2,1,0:T(8,128)(2,1)}, u32[]{:S(2)}, u32[]{:S(2)}) collective-permute-start(bf16[2,336,512]{2,1,0:T(8,128)(2,1)S(1)} %pad_maximum_fusion.refs_0_), channel_id=1, source_target_pairs={{0,16},{16,0},{1,17},{17,1},{2,18},{18,2},{3,19},{19,3},{4,20},{20... | collective-permute-start | bytes 2064392 | tf_op jit(solution)/shard_map/ppermute | solution.py:35
  44.8 1.1 collective-permute-start.17
  45.9 2.1 %collective-permute-start.18 = (bf16[336,512]{1,0:T(8,128)(2,1)}, bf16[336,512]{1,0:T(8,128)(2,1)S(1)}, u32[]{:S(2)}, u32[]{:S(2)}) collective-permute-start(bf16[336,512]{1,0:T(8,128)(2,1)} %copy-done.2), channel_id=1, source_target_pairs={{0,14},{2,0},{4,2},{6,4},{8,6},{10,8},{12,10},{14,12},{1,15},{3,1}... | collective-permute-start | bytes 1032200 | tf_op jit(solution)/shard_map/ppermute | solution.py:31
  48.0 0.0 collective-permute-start.14
  48.0 8.5 %collective-permute-done.17.refs_5_ = bf16[336,512]{1,0:T(8,128)(2,1)} collective-permute-done((bf16[336,512]{1,0:T(8,128)(2,1)}, bf16[336,512]{1,0:T(8,128)(2,1)}, u32[]{:S(2)}, u32[]{:S(2)}) %collective-permute-start.17) | collective-permute-done | bytes 344096 | tf_op jit(solution)/shard_map/ppermute | solution.py:31
  56.5 0.5 collective-permute-start.15
  57.0 0.7 copy-done.4
  57.7 2.3 %collective-permute-start.22 = (bf16[336,512]{1,0:T(8,128)(2,1)}, bf16[336,512]{1,0:T(8,128)(2,1)}, u32[]{:S(2)}, u32[]{:S(2)}) collective-permute-start(bf16[336,512]{1,0:T(8,128)(2,1)} %collective-permute-done.9.refs_4_), channel_id=1, source_target_pairs={{0,14},{2,0},{4,2},{6,4},{8,6},{10,8},{12,10},{14,12},{1,15},{3,1}... | collective-permute-start | bytes 1032200 | tf_op jit(solution)/shard_map/ppermute | solution.py:31
  60.1 0.0 collective-permute-done.13.refs_4_
  60.1 0.0 collective-permute-start.19
  60.1 0.1 pad_add_fusion.where_ref
  60.1 7.9 %collective-permute-done.22.refs_6_ = bf16[336,512]{1,0:T(8,128)(2,1)} collective-permute-done((bf16[336,512]{1,0:T(8,128)(2,1)}, bf16[336,512]{1,0:T(8,128)(2,1)}, u32[]{:S(2)}, u32[]{:S(2)}) %collective-permute-start.22) | collective-permute-done | bytes 344096 | tf_op jit(solution)/shard_map/ppermute | solution.py:31
  68.0 0.9 collective-permute-start.21
  68.9 2.4 %collective-permute-start.23 = (bf16[336,512]{1,0:T(8,128)(2,1)}, bf16[336,512]{1,0:T(8,128)(2,1)S(1)}, u32[]{:S(2)}, u32[]{:S(2)}) collective-permute-start(bf16[336,512]{1,0:T(8,128)(2,1)} %collective-permute-done.22.refs_6_), channel_id=1, source_target_pairs={{0,14},{2,0},{4,2},{6,4},{8,6},{10,8},{12,10},{14,12},{1,15},{3,1}... | collective-permute-start | bytes 1032200 | tf_op jit(solution)/shard_map/ppermute | solution.py:31
  71.3 1.1 fusion.2
  72.4 2.7 %shard_map.28.weights_ref = bf16[8,336,1024]{2,1,0:T(8,128)(2,1)S(1)} custom-call(s32[3]{0:T(128)S(1)} %pad_add_fusion.where_ref, bf16[2,336,512]{2,1,0:T(8,128)(2,1)S(1)} %pad_maximum_fusion.refs_0_, bf16[2,336,512]{2,1,0:T(8,128)(2,1)S(1)} %collective-permute-done.10.refs_1_, bf16[2,336,512]{2,1,0:T(8,128)(2,1)} %collective-permute-done.12.refs_2_, ...), custom_call_target="tpu_custom_call" | custom-call | bytes 5505024 | tf_op jit(solution)/shard_map/pallas_call | solution.py:119
  75.1 2.7 %shard_map.29 = bf16[512,512]{1,0:T(8,128)(2,1)S(1)} custom-call(s32[1]{0:T(128)} %bitcast.1.z_ref, bf16[8,336,1024]{2,1,0:T(8,128)(2,1)S(1)} %shard_map.28.weights_ref, bf16[336,512]{1,0:T(8,128)(2,1)S(1)} %get-tuple-element.70.refs_0_, bf16[336,512]{1,0:T(8,128)(2,1)S(1)} %collective-permute-done.refs_1_, ...), custom_call_target="tpu_custom_call" | custom-call | flops 1409286144 | bytes 5505024 | tf_op jit(solution)/shard_map/pallas_call | solution.py:148
  77.8 0.1 collective-permute-start.20
  77.9 0.6 collective-permute-done.21.refs_5_
  78.6 3.1 %shard_map.30 = bf16[512,512]{1,0:T(8,128)(2,1)S(1)} custom-call(s32[1]{0:T(128)} %bitcast.1.z_ref, bf16[8,336,1024]{2,1,0:T(8,128)(2,1)S(1)} %shard_map.28.weights_ref, bf16[336,512]{1,0:T(8,128)(2,1)S(1)} %get-tuple-element.69.refs_0_, bf16[336,512]{1,0:T(8,128)(2,1)} %collective-permute-done.6.refs_1_, bf16[336,512]{1,0:T(8,128)(2,1)} %collective-permute-done.7.refs_2_, ...), custom_call_target="tpu_custom_call" | custom-call | flops 1409286144 | bytes 5505024 | tf_op jit(solution)/shard_map/pallas_call | solution.py:148
  81.7 3.2 %collective-permute-start.24 = (bf16[512,512]{1,0:T(8,128)(2,1)S(1)}, bf16[512,512]{1,0:T(8,128)(2,1)S(1)}, u32[]{:S(2)}, u32[]{:S(2)}) collective-permute-start(bf16[512,512]{1,0:T(8,128)(2,1)S(1)} %shard_map.30), channel_id=1, source_target_pairs={{0,1},{1,0},{2,3},{3,2},{4,5},{5,4},{6,7},{7,6},{8,9},{9,8},{10,11... | collective-permute-start | bytes 1572872 | tf_op jit(solution)/shard_map/ppermute | solution.py:35
  84.9 2.7 %shard_map.31.keep_ref = f32[512,512]{1,0:T(8,128)S(1)} custom-call(s32[1]{0:T(128)} %bitcast.1.z_ref, bf16[8,336,1024]{2,1,0:T(8,128)(2,1)S(1)} %shard_map.28.weights_ref, bf16[336,512]{1,0:T(8,128)(2,1)S(1)} %get-tuple-element.70.refs_0_, bf16[336,512]{1,0:T(8,128)(2,1)S(1)} %collective-permute-done.refs_1_, ...), custom_call_target="tpu_custom_call" | custom-call | flops 1409286144 | bytes 5505024 | tf_op jit(solution)/shard_map/pallas_call | solution.py:148
  87.6 3.1 %shard_map.32.keep_ref = f32[512,512]{1,0:T(8,128)S(1)} custom-call(s32[1]{0:T(128)} %bitcast.1.z_ref, bf16[8,336,1024]{2,1,0:T(8,128)(2,1)S(1)} %shard_map.28.weights_ref, bf16[336,512]{1,0:T(8,128)(2,1)S(1)} %get-tuple-element.69.refs_0_, bf16[336,512]{1,0:T(8,128)(2,1)} %collective-permute-done.6.refs_1_, ...), custom_call_target="tpu_custom_call" | custom-call | flops 1409286144 | bytes 5505024 | tf_op jit(solution)/shard_map/pallas_call | solution.py:148
  90.7 3.6 %collective-permute-done.20.sent_ref = bf16[512,512]{1,0:T(8,128)(2,1)S(1)} collective-permute-done((bf16[512,512]{1,0:T(8,128)(2,1)S(1)}, bf16[512,512]{1,0:T(8,128)(2,1)S(1)}, u32[]{:S(2)}, u32[]{:S(2)}) %collective-permute-start.20) | collective-permute-done | bytes 524320 | tf_op jit(solution)/shard_map/ppermute | solution.py:35
  94.3 0.3 shard_map.34
  94.6 1.9 %collective-permute-start.26 = (bf16[512,256]{1,0:T(8,128)(2,1)S(1)}, bf16[512,256]{1,0:T(8,128)(2,1)S(1)}, u32[]{:S(2)}, u32[]{:S(2)}) collective-permute-start(bf16[512,256]{1,0:T(8,128)(2,1)S(1)} %get-tuple-element.61.refs_1_), channel_id=1, source_target_pairs={{0,16},{16,32},{32,48},{48,64},{64,80},{80,96},{96,112},{112,128},... | collective-permute-start | bytes 786440 | tf_op jit(solution)/shard_map/ppermute | solution.py:311
  96.5 6.5 %collective-permute-done.24.sent_ref = bf16[512,512]{1,0:T(8,128)(2,1)S(1)} collective-permute-done((bf16[512,512]{1,0:T(8,128)(2,1)S(1)}, bf16[512,512]{1,0:T(8,128)(2,1)S(1)}, u32[]{:S(2)}, u32[]{:S(2)}) %collective-permute-start.24) | collective-permute-done | bytes 524320 | tf_op jit(solution)/shard_map/ppermute | solution.py:35
  103.1 0.3 shard_map.33
  103.4 1.9 %collective-permute-start.25 = (bf16[512,256]{1,0:T(8,128)(2,1)S(1)}, bf16[512,256]{1,0:T(8,128)(2,1)S(1)}, u32[]{:S(2)}, u32[]{:S(2)}) collective-permute-start(bf16[512,256]{1,0:T(8,128)(2,1)S(1)} %get-tuple-element.58.refs_1_.refs_0_), channel_id=1, source_target_pairs={{0,16},{16,32},{32,48},{48,64},{64,80},{80,96},{96,112},{112,128},... | collective-permute-start | bytes 786440 | tf_op jit(solution)/shard_map/ppermute | solution.py:313
  105.3 1.6 %shard_map.36 = (f32[1024,128]{1,0:T(8,128)S(1)}, f32[1024,128]{1,0:T(8,128)S(1)}, f32[1024,128]{1,0:T(8,128)S(1)}) custom-call(s32[1]{0:T(128)} %bitcast.first_ref, bf16[512,256]{1,0:T(8,128)(2,1)S(1)} %get-tuple-element.65.q_ref, bf16[512,256]{1,0:T(8,128)(2,1)S(1)} %collective-permute-done.26.refs_0_, bf16[512,256]{1,0:T(8,128)(2,1)S(1)} %get-tuple-element.61.refs_1_), custom_call_target="tpu_custom_call" | custom-call | flops 402653184 | bytes 2097152 | tf_op jit(solution)/shard_map/pallas_call | solution.py:262
  106.9 1.1 shard_map.37.refs_4_
  108.0 2.0 %shard_map.35 = (f32[1024,128]{1,0:T(8,128)S(1)}, f32[1024,128]{1,0:T(8,128)S(1)}, f32[1024,128]{1,0:T(8,128)S(1)}) custom-call(s32[1]{0:T(128)} %bitcast.first_ref, bf16[512,256]{1,0:T(8,128)(2,1)S(1)} %get-tuple-element.57.q_ref, bf16[512,256]{1,0:T(8,128)(2,1)S(1)} %collective-permute-done.26.refs_0_, bf16[512,256]{1,0:T(8,128)(2,1)S(1)} %get-tuple-element.58.refs_1_.refs_0_), custom_call_target="tpu_custom_call" | custom-call | flops 469762048 | bytes 2097152 | tf_op jit(solution)/shard_map/pallas_call | solution.py:262
  110.0 3.2 %collective-permute-done.25.refs_0_ = bf16[512,256]{1,0:T(8,128)(2,1)S(1)} collective-permute-done((bf16[512,256]{1,0:T(8,128)(2,1)S(1)}, bf16[512,256]{1,0:T(8,128)(2,1)S(1)}, u32[]{:S(2)}, u32[]{:S(2)}) %collective-permute-start.25) | collective-permute-done | bytes 262176 | tf_op jit(solution)/shard_map/ppermute | solution.py:313
  113.2 1.7 %shard_map.38 = bf16[1024,256]{1,0:T(8,128)(2,1)} custom-call(s32[1]{0:T(128)} %bitcast.first_ref, bf16[512,256]{1,0:T(8,128)(2,1)S(1)} %get-tuple-element.57.q_ref, bf16[512,256]{1,0:T(8,128)(2,1)S(1)} %collective-permute-done.25.refs_0_, f32[1024,128]{1,0:T(8,128)S(1)} %get-tuple-element.62.refs_1_, f32[1024,128]{1,0:T(8,128)S(1)} %get-tuple-element.63.refs_2_, ...), custom_call_target="tpu_custom_call" | custom-call | flops 201326592 | bytes 2097152 | tf_op jit(solution)/shard_map/pallas_call | solution.py:262
  (28 shorter events, 0.1 us)
Async XLA Ops:
  0.0 15.0 %copy-start.7 = (bf16[336,512]{1,0:T(8,128)(2,1)S(1)}, bf16[336,512]{1,0:T(8,128)(2,1)}, u32[]{:S(2)}) copy-start(bf16[336,512]{1,0:T(8,128)(2,1)} %param.3) | copy-start | bytes 1032196
  1.2 14.3 %collective-permute-start = (bf16[336,512]{1,0:T(8,128)(2,1)S(1)}, bf16[336,512]{1,0:T(8,128)(2,1)S(1)}, u32[]{:S(2)}, u32[]{:S(2)}) collective-permute-start(bf16[336,512]{1,0:T(8,128)(2,1)S(1)} %get-tuple-element.70.refs_0_), channel_id=1, source_target_pairs={{0,2},{2,4},{4,6},{6,8},{8,10},{10,12},{12,14},{14,0},{1,3},{3,5},... | collective-permute-start | bytes 1032200 | tf_op jit(solution)/shard_map/ppermute | solution.py:31
  3.2 12.3 %collective-permute-start.1 = (bf16[336,512]{1,0:T(8,128)(2,1)S(1)}, bf16[336,512]{1,0:T(8,128)(2,1)S(1)}, u32[]{:S(2)}, u32[]{:S(2)}) collective-permute-start(bf16[336,512]{1,0:T(8,128)(2,1)S(1)} %get-tuple-element.70.refs_0_), channel_id=1, source_target_pairs={{0,14},{2,0},{4,2},{6,4},{8,6},{10,8},{12,10},{14,12},{1,15},{3,1}... | collective-permute-start | bytes 1032200 | tf_op jit(solution)/shard_map/ppermute | solution.py:31
  7.2 8.2 %collective-permute-start.3 = (bf16[336,512]{1,0:T(8,128)(2,1)}, bf16[336,512]{1,0:T(8,128)(2,1)S(1)}, u32[]{:S(2)}, u32[]{:S(2)}) collective-permute-start(bf16[336,512]{1,0:T(8,128)(2,1)} %param.3), channel_id=1, source_target_pairs={{0,128},{1,144},{16,129},{17,145},{128,0},{129,16},{144,1},{145,17... | collective-permute-start | bytes 1032200 | tf_op jit(solution)/shard_map/ppermute | solution.py:59
  7.7 4.0 %collective-permute-start.2 = (bf16[336,512]{1,0:T(8,128)(2,1)}, bf16[336,512]{1,0:T(8,128)(2,1)S(1)}, u32[]{:S(2)}, u32[]{:S(2)}) collective-permute-start(bf16[336,512]{1,0:T(8,128)(2,1)} %param.3), channel_id=1, source_target_pairs={{1,16},{16,1},{3,18},{18,3},{5,20},{20,5},{7,22},{22,7},{9,24},{24... | collective-permute-start | bytes 1032200 | tf_op jit(solution)/shard_map/ppermute | solution.py:52
  8.4 14.1 %collective-permute-start.6 = (bf16[336,512]{1,0:T(8,128)(2,1)S(1)}, bf16[336,512]{1,0:T(8,128)(2,1)}, u32[]{:S(2)}, u32[]{:S(2)}) collective-permute-start(bf16[336,512]{1,0:T(8,128)(2,1)S(1)} %get-tuple-element.69.refs_0_), channel_id=1, source_target_pairs={{0,2},{2,4},{4,6},{6,8},{8,10},{10,12},{12,14},{14,0},{1,3},{3,5},... | collective-permute-start | bytes 1032200 | tf_op jit(solution)/shard_map/ppermute | solution.py:31
  11.8 13.8 %collective-permute-start.7 = (bf16[336,512]{1,0:T(8,128)(2,1)S(1)}, bf16[336,512]{1,0:T(8,128)(2,1)}, u32[]{:S(2)}, u32[]{:S(2)}) collective-permute-start(bf16[336,512]{1,0:T(8,128)(2,1)S(1)} %get-tuple-element.69.refs_0_), channel_id=1, source_target_pairs={{0,14},{2,0},{4,2},{6,4},{8,6},{10,8},{12,10},{14,12},{1,15},{3,1}... | collective-permute-start | bytes 1032200 | tf_op jit(solution)/shard_map/ppermute | solution.py:31
  15.5 11.7 %collective-permute-start.4 = (bf16[336,512]{1,0:T(8,128)(2,1)S(1)}, bf16[336,512]{1,0:T(8,128)(2,1)S(1)}, u32[]{:S(2)}, u32[]{:S(2)}) collective-permute-start(bf16[336,512]{1,0:T(8,128)(2,1)S(1)} %collective-permute-done.refs_1_), channel_id=1, source_target_pairs={{0,2},{2,4},{4,6},{6,8},{8,10},{10,12},{12,14},{14,0},{1,3},{3,5},... | collective-permute-start | bytes 1032200 | tf_op jit(solution)/shard_map/ppermute | solution.py:31
  15.6 11.6 %collective-permute-start.5 = (bf16[336,512]{1,0:T(8,128)(2,1)S(1)}, bf16[336,512]{1,0:T(8,128)(2,1)S(1)}, u32[]{:S(2)}, u32[]{:S(2)}) collective-permute-start(bf16[336,512]{1,0:T(8,128)(2,1)S(1)} %collective-permute-done.1.refs_2_), channel_id=1, source_target_pairs={{0,14},{2,0},{4,2},{6,4},{8,6},{10,8},{12,10},{14,12},{1,15},{3,1}... | collective-permute-start | bytes 1032200 | tf_op jit(solution)/shard_map/ppermute | solution.py:31
  18.8 20.9 %collective-permute-start.10 = (bf16[2,336,512]{2,1,0:T(8,128)(2,1)S(1)}, bf16[2,336,512]{2,1,0:T(8,128)(2,1)S(1)}, u32[]{:S(2)}, u32[]{:S(2)}) collective-permute-start(bf16[2,336,512]{2,1,0:T(8,128)(2,1)S(1)} %pad_maximum_fusion.refs_0_), channel_id=1, source_target_pairs={{0,32},{32,64},{64,96},{96,0},{1,33},{33,65},{65,97},{97,1},{2,34}... | collective-permute-start | bytes 2064392 | tf_op jit(solution)/shard_map/ppermute | solution.py:31
  22.5 18.3 %collective-permute-start.11 = (bf16[2,336,512]{2,1,0:T(8,128)(2,1)S(1)}, bf16[2,336,512]{2,1,0:T(8,128)(2,1)S(1)}, u32[]{:S(2)}, u32[]{:S(2)}) collective-permute-start(bf16[2,336,512]{2,1,0:T(8,128)(2,1)S(1)} %pad_maximum_fusion.refs_0_), channel_id=1, source_target_pairs={{0,96},{32,0},{64,32},{96,64},{1,97},{33,1},{65,33},{97,65},{2,98}... | collective-permute-start | bytes 2064392 | tf_op jit(solution)/shard_map/ppermute | solution.py:31
  27.2 0.7 copy-start
  28.0 1.9 %copy-start.2 = (bf16[336,512]{1,0:T(8,128)(2,1)}, bf16[336,512]{1,0:T(8,128)(2,1)S(1)}, u32[]{:S(2)}) copy-start(bf16[336,512]{1,0:T(8,128)(2,1)S(1)} %collective-permute-done.5.refs_4_) | copy-start | bytes 1032196
  28.0 11.2 %collective-permute-start.8 = (bf16[336,512]{1,0:T(8,128)(2,1)}, bf16[336,512]{1,0:T(8,128)(2,1)}, u32[]{:S(2)}, u32[]{:S(2)}) collective-permute-start(bf16[336,512]{1,0:T(8,128)(2,1)} %collective-permute-done.6.refs_1_), channel_id=1, source_target_pairs={{0,2},{2,4},{4,6},{6,8},{8,10},{10,12},{12,14},{14,0},{1,3},{3,5},... | collective-permute-start | bytes 1032200 | tf_op jit(solution)/shard_map/ppermute | solution.py:31
  29.9 9.8 %collective-permute-start.9 = (bf16[336,512]{1,0:T(8,128)(2,1)}, bf16[336,512]{1,0:T(8,128)(2,1)}, u32[]{:S(2)}, u32[]{:S(2)}) collective-permute-start(bf16[336,512]{1,0:T(8,128)(2,1)} %collective-permute-done.7.refs_2_), channel_id=1, source_target_pairs={{0,14},{2,0},{4,2},{6,4},{8,6},{10,8},{12,10},{14,12},{1,15},{3,1}... | collective-permute-start | bytes 1032200 | tf_op jit(solution)/shard_map/ppermute | solution.py:31
  40.9 15.6 %collective-permute-start.12 = (bf16[2,336,512]{2,1,0:T(8,128)(2,1)S(1)}, bf16[2,336,512]{2,1,0:T(8,128)(2,1)}, u32[]{:S(2)}, u32[]{:S(2)}) collective-permute-start(bf16[2,336,512]{2,1,0:T(8,128)(2,1)S(1)} %broadcast_select_fusion), channel_id=1, source_target_pairs={{0,32},{16,112},{32,64},{48,16},{64,96},{80,48},{96,0},{112,80},{1... | collective-permute-start | bytes 2064392 | tf_op jit(solution)/shard_map/ppermute | solution.py:74
  41.7 18.3 %collective-permute-start.13 = (bf16[2,336,512]{2,1,0:T(8,128)(2,1)S(1)}, bf16[2,336,512]{2,1,0:T(8,128)(2,1)}, u32[]{:S(2)}, u32[]{:S(2)}) collective-permute-start(bf16[2,336,512]{2,1,0:T(8,128)(2,1)S(1)} %pad_maximum_fusion.refs_0_), channel_id=1, source_target_pairs={{0,16},{16,0},{1,17},{17,1},{2,18},{18,2},{3,19},{19,3},{4,20},{20... | collective-permute-start | bytes 2064392 | tf_op jit(solution)/shard_map/ppermute | solution.py:35
  44.8 11.7 %collective-permute-start.17 = (bf16[336,512]{1,0:T(8,128)(2,1)}, bf16[336,512]{1,0:T(8,128)(2,1)}, u32[]{:S(2)}, u32[]{:S(2)}) collective-permute-start(bf16[336,512]{1,0:T(8,128)(2,1)} %copy-done), channel_id=1, source_target_pairs={{0,2},{2,4},{4,6},{6,8},{8,10},{10,12},{12,14},{14,0},{1,3},{3,5},... | collective-permute-start | bytes 1032200 | tf_op jit(solution)/shard_map/ppermute | solution.py:31
  45.9 11.1 %collective-permute-start.18 = (bf16[336,512]{1,0:T(8,128)(2,1)}, bf16[336,512]{1,0:T(8,128)(2,1)S(1)}, u32[]{:S(2)}, u32[]{:S(2)}) collective-permute-start(bf16[336,512]{1,0:T(8,128)(2,1)} %copy-done.2), channel_id=1, source_target_pairs={{0,14},{2,0},{4,2},{6,4},{8,6},{10,8},{12,10},{14,12},{1,15},{3,1}... | collective-permute-start | bytes 1032200 | tf_op jit(solution)/shard_map/ppermute | solution.py:31
  48.0 20.9 %collective-permute-start.14 = (bf16[2,336,512]{2,1,0:T(8,128)(2,1)S(1)}, bf16[2,336,512]{2,1,0:T(8,128)(2,1)}, u32[]{:S(2)}, u32[]{:S(2)}) collective-permute-start(bf16[2,336,512]{2,1,0:T(8,128)(2,1)S(1)} %collective-permute-done.10.refs_1_), channel_id=1, source_target_pairs={{0,16},{16,0},{1,17},{17,1},{2,18},{18,2},{3,19},{19,3},{4,20},{20... | collective-permute-start | bytes 2064392 | tf_op jit(solution)/shard_map/ppermute | solution.py:35
  56.5 15.9 %collective-permute-start.16 = (bf16[2,336,512]{2,1,0:T(8,128)(2,1)S(1)}, bf16[2,336,512]{2,1,0:T(8,128)(2,1)}, u32[]{:S(2)}, u32[]{:S(2)}) collective-permute-start(bf16[2,336,512]{2,1,0:T(8,128)(2,1)S(1)} %collective-permute-done.11.refs_3_), channel_id=1, source_target_pairs={{0,16},{16,0},{1,17},{17,1},{2,18},{18,2},{3,19},{19,3},{4,20},{20... | collective-permute-start | bytes 2064392 | tf_op jit(solution)/shard_map/ppermute | solution.py:35
  56.5 15.9 %collective-permute-start.15 = (bf16[2,336,512]{2,1,0:T(8,128)(2,1)}, bf16[2,336,512]{2,1,0:T(8,128)(2,1)}, u32[]{:S(2)}, u32[]{:S(2)}) collective-permute-start(bf16[2,336,512]{2,1,0:T(8,128)(2,1)} %collective-permute-done.12.refs_2_), channel_id=1, source_target_pairs={{0,16},{16,0},{1,17},{17,1},{2,18},{18,2},{3,19},{19,3},{4,20},{20... | collective-permute-start | bytes 2064392 | tf_op jit(solution)/shard_map/ppermute | solution.py:35
  57.0 0.7 copy-start.4
  57.7 10.3 %collective-permute-start.22 = (bf16[336,512]{1,0:T(8,128)(2,1)}, bf16[336,512]{1,0:T(8,128)(2,1)}, u32[]{:S(2)}, u32[]{:S(2)}) collective-permute-start(bf16[336,512]{1,0:T(8,128)(2,1)} %collective-permute-done.9.refs_4_), channel_id=1, source_target_pairs={{0,14},{2,0},{4,2},{6,4},{8,6},{10,8},{12,10},{14,12},{1,15},{3,1}... | collective-permute-start | bytes 1032200 | tf_op jit(solution)/shard_map/ppermute | solution.py:31
  60.1 15.0 %collective-permute-start.19 = (bf16[336,512]{1,0:T(8,128)(2,1)}, bf16[336,512]{1,0:T(8,128)(2,1)S(1)}, u32[]{:S(2)}, u32[]{:S(2)}) collective-permute-start(bf16[336,512]{1,0:T(8,128)(2,1)} %collective-permute-done.17.refs_5_), channel_id=1, source_target_pairs={{0,2},{2,4},{4,6},{6,8},{8,10},{10,12},{12,14},{14,0},{1,3},{3,5},... | collective-permute-start | bytes 1032200 | tf_op jit(solution)/shard_map/ppermute | solution.py:31
  68.0 10.5 %collective-permute-start.21 = (bf16[336,512]{1,0:T(8,128)(2,1)}, bf16[336,512]{1,0:T(8,128)(2,1)S(1)}, u32[]{:S(2)}, u32[]{:S(2)}) collective-permute-start(bf16[336,512]{1,0:T(8,128)(2,1)} %collective-permute-done.8.refs_3_), channel_id=1, source_target_pairs={{0,2},{2,4},{4,6},{6,8},{8,10},{10,12},{12,14},{14,0},{1,3},{3,5},... | collective-permute-start | bytes 1032200 | tf_op jit(solution)/shard_map/ppermute | solution.py:31
  68.9 9.7 %collective-permute-start.23 = (bf16[336,512]{1,0:T(8,128)(2,1)}, bf16[336,512]{1,0:T(8,128)(2,1)S(1)}, u32[]{:S(2)}, u32[]{:S(2)}) collective-permute-start(bf16[336,512]{1,0:T(8,128)(2,1)} %collective-permute-done.22.refs_6_), channel_id=1, source_target_pairs={{0,14},{2,0},{4,2},{6,4},{8,6},{10,8},{12,10},{14,12},{1,15},{3,1}... | collective-permute-start | bytes 1032200 | tf_op jit(solution)/shard_map/ppermute | solution.py:31
  72.3 2.8 %copy-start.1 = (bf16[336,512]{1,0:T(8,128)(2,1)S(1)}, bf16[336,512]{1,0:T(8,128)(2,1)}, u32[]{:S(2)}) copy-start(bf16[336,512]{1,0:T(8,128)(2,1)} %copy-done) | copy-start | bytes 1032196
  72.3 2.8 %copy-start.3 = (bf16[336,512]{1,0:T(8,128)(2,1)S(1)}, bf16[336,512]{1,0:T(8,128)(2,1)}, u32[]{:S(2)}) copy-start(bf16[336,512]{1,0:T(8,128)(2,1)} %copy-done.2) | copy-start | bytes 1032196
  72.3 2.8 %copy-start.5 = (bf16[336,512]{1,0:T(8,128)(2,1)S(1)}, bf16[336,512]{1,0:T(8,128)(2,1)}, u32[]{:S(2)}) copy-start(bf16[336,512]{1,0:T(8,128)(2,1)} %copy-done.4) | copy-start | bytes 1032196
  77.8 7.1 %copy-start.6 = (f32[1024,128]{1,0:T(8,128)S(1)}, f32[1024,128]{1,0:T(8,128)}, u32[]{:S(2)}) copy-start(f32[1024,128]{1,0:T(8,128)} %get-tuple-element.56) | copy-start | bytes 1572868
  77.8 16.5 %collective-permute-start.20 = (bf16[512,512]{1,0:T(8,128)(2,1)S(1)}, bf16[512,512]{1,0:T(8,128)(2,1)S(1)}, u32[]{:S(2)}, u32[]{:S(2)}) collective-permute-start(bf16[512,512]{1,0:T(8,128)(2,1)S(1)} %shard_map.29), channel_id=1, source_target_pairs={{0,1},{1,0},{2,3},{3,2},{4,5},{5,4},{6,7},{7,6},{8,9},{9,8},{10,11... | collective-permute-start | bytes 1572872 | tf_op jit(solution)/shard_map/ppermute | solution.py:35
  81.7 21.4 %collective-permute-start.24 = (bf16[512,512]{1,0:T(8,128)(2,1)S(1)}, bf16[512,512]{1,0:T(8,128)(2,1)S(1)}, u32[]{:S(2)}, u32[]{:S(2)}) collective-permute-start(bf16[512,512]{1,0:T(8,128)(2,1)S(1)} %shard_map.30), channel_id=1, source_target_pairs={{0,1},{1,0},{2,3},{3,2},{4,5},{5,4},{6,7},{7,6},{8,9},{9,8},{10,11... | collective-permute-start | bytes 1572872 | tf_op jit(solution)/shard_map/ppermute | solution.py:35
  94.6 10.7 %collective-permute-start.26 = (bf16[512,256]{1,0:T(8,128)(2,1)S(1)}, bf16[512,256]{1,0:T(8,128)(2,1)S(1)}, u32[]{:S(2)}, u32[]{:S(2)}) collective-permute-start(bf16[512,256]{1,0:T(8,128)(2,1)S(1)} %get-tuple-element.61.refs_1_), channel_id=1, source_target_pairs={{0,16},{16,32},{32,48},{48,64},{64,80},{80,96},{96,112},{112,128},... | collective-permute-start | bytes 786440 | tf_op jit(solution)/shard_map/ppermute | solution.py:311
  103.4 9.8 %collective-permute-start.25 = (bf16[512,256]{1,0:T(8,128)(2,1)S(1)}, bf16[512,256]{1,0:T(8,128)(2,1)S(1)}, u32[]{:S(2)}, u32[]{:S(2)}) collective-permute-start(bf16[512,256]{1,0:T(8,128)(2,1)S(1)} %get-tuple-element.58.refs_1_.refs_0_), channel_id=1, source_target_pairs={{0,16},{16,32},{32,48},{48,64},{64,80},{80,96},{96,112},{112,128},... | collective-permute-start | bytes 786440 | tf_op jit(solution)/shard_map/ppermute | solution.py:313

commit v3 on v2

--- a/solution.py
+++ b/solution.py
@@ -128,7 +128,7 @@
 
 
 def product_kernel(half, z_ref, weights_ref, *refs):
-    tokens, out_ref = refs[:-1], refs[-1]
+    tokens, outs = refs[:8], refs[8:]
     z = z_ref[0]
     width = weights_ref.shape[-1] // 2
     lhs = jnp.concatenate([t[...] for t in tokens], axis=0)
@@ -138,18 +138,20 @@
     total = lax.dot_general(
         lhs, rhs, (((0,), (0,)), ((), ())), preferred_element_type=jnp.float32
     )
-    out_ref[...] = total.astype(out_ref.dtype)
-
-
-def product(z, shards, weights, half, dtype):
+    part = width // len(outs)
+    for i, out_ref in enumerate(outs):
+        out_ref[...] = total[:, i * part : (i + 1) * part].astype(out_ref.dtype)
+
+
+def product(z, shards, weights, half, dtype, parts=1):
     depth, rows = shards[0].shape
     width = weights.shape[-1] // 2
     vmem = pl.BlockSpec(memory_space=pltpu.VMEM)
     return pl.pallas_call(
         functools.partial(product_kernel, half),
-        out_shape=jax.ShapeDtypeStruct((rows, width), dtype),
+        out_shape=[jax.ShapeDtypeStruct((rows, width // parts), dtype)] * parts,
         in_specs=[pl.BlockSpec(memory_space=pltpu.SMEM)] + [vmem] * 9,
-        out_specs=vmem,
+        out_specs=[vmem] * parts,
         compiler_params=pltpu.CompilerParams(vmem_limit_bytes=VMEM_BYTES),
         cost_estimate=pl.CostEstimate(
             flops=2 * 8 * depth * rows * width,
@@ -184,6 +186,31 @@
         compiler_params=pltpu.CompilerParams(vmem_limit_bytes=VMEM_BYTES),
         cost_estimate=pl.CostEstimate(
             flops=rows * 2048, bytes_accessed=rows * 6000, transcendentals=0
+        ),
+    )(keep, sent, cos, sin)
+
+
+def finish_pair_kernel(start, turns, keep_ref, sent_ref, cos_ref, sin_ref, out_ref):
+    for j, turn in enumerate(turns):
+        columns = pl.ds(j * HEAD, HEAD)
+        block = keep_ref[:, pl.ds((start + j) * HEAD, HEAD)]
+        block = block + sent_ref[:, columns].astype(jnp.float32)
+        if turn:
+            block = block * cos_ref[...] + pltpu.roll(block, HEAD // 2, 1) * sin_ref[...]
+        out_ref[:, columns] = block.astype(jnp.bfloat16)
+
+
+def finish_pair(keep, sent, cos, sin, start, turns):
+    rows = keep.shape[0]
+    vmem = pl.BlockSpec(memory_space=pltpu.VMEM)
+    return pl.pallas_call(
+        functools.partial(finish_pair_kernel, start, turns),
+        out_shape=jax.ShapeDtypeStruct((rows, 2 * HEAD), jnp.bfloat16),
+        in_specs=[vmem] * 4,
+        out_specs=vmem,
+        compiler_params=pltpu.CompilerParams(vmem_limit_bytes=VMEM_BYTES),
+        cost_estimate=pl.CostEstimate(
+            flops=rows * 1024, bytes_accessed=rows * 3000, transcendentals=0
         ),
     )(keep, sent, cos, sin)
 
@@ -299,17 +326,20 @@
     )
 
     tie = lax.optimization_barrier
-    send_high = product(z_place, shards[0], weights, 1, jnp.bfloat16)
+    (send_high,) = product(z_place, shards[0], weights, 1, jnp.bfloat16)
     sent_high = swap(send_high, "x_hi")
     send_high, z_place = tie((send_high, z_place))
-    send_low = product(z_place, shards[1], weights, 1, jnp.bfloat16)
-    sent_low = swap(send_low, "x_hi")
-    send_low, z_place = tie((send_low, z_place))
-    keep_high, keep_low = (product(z_place, s, weights, 0, jnp.float32) for s in shards)
+    send_q, send_kv = product(z_place, shards[1], weights, 1, jnp.bfloat16, 2)
+    sent_kv = swap(send_kv, "x_hi")
+    send_kv, z_place = tie((send_kv, z_place))
+    keep_high, keep_low = (product(z_place, s, weights, 0, jnp.float32)[0] for s in shards)
+    send_q, keep_high = tie((send_q, keep_high))
+    sent_q = swap(send_q, "x_hi")
     sent_high, keep_high, keep_low = tie((sent_high, keep_high, keep_low))
     q_high, own_high = finish(keep_high, sent_high, cos[rows:], sin[rows:])
     before_high = lax.ppermute(own_high, CTX, [(c, c + 1) for c in range(15)])
-    q_low, own_low = finish(keep_low, sent_low, cos[:rows], sin[:rows])
+    own_low = finish_pair(keep_low, sent_kv, cos[:rows], sin[:rows], 2, (True, False))
+    q_low = finish_pair(keep_low, sent_q, cos[:rows], sin[:rows], 0, (True, True))
     before_low = lax.ppermute(own_low, CTX, [(c, c + 1) for c in range(15)])
 
     first = ctx.astype(jnp.int32)[None]

time: 115 us -> 110 us (0.957)
  waiting for transfers between devices: 42.7 us -> 37.4 us
    ppermute x6 -> x7, waiting for transfers between devices: 10.1 us -> 6.48 us  [swap(): return lax.ppermute(block, axis, [(0, 1), (1, 0)])]
    ppermute x1, waiting for transfers between devices: 3.18 us -> 0.16 us  [on_device(): before_low = lax.ppermute(own_low, CTX, [(c, c + 1) for c in range(15)])]
    ppermute x1, waiting for transfers between devices: 0.01 us -> 1.65 us  [on_device(): before_high = lax.ppermute(own_high, CTX, [(c, c + 1) for c in range(15)])]
    ppermute x6 -> x7, starting transfers between devices: 6.83 us -> 7.62 us  [swap(): return lax.ppermute(block, axis, [(0, 1), (1, 0)])]
    pallas_call x4 -> x6, Pallas kernels: 11.6 us -> 12 us  [the longest x4 11.6 us: product(): pl.pallas_call(functools.partial(product_kernel, half), out_shape=[jax.Sh...]
  transfers between devices with their start and end apart: 27 -> 28, of which waited for: 12 -> 14; matrix products, arithmetic and copies ran while one was open for 4% -> 4% of each run, Pallas kernels for 17% -> 18%
where the time goes in v3:
time: 110 us
  starting transfers between devices  44.4 us (40%)
  waiting for transfers between devices  37.4 us (34%)
  Pallas kernels  21.4 us (19%)
  other arithmetic  3.46 us (3%)
  local copies, waits for them, and re-layouts  3.02 us (3%)
    ppermute x16, starting transfers between devices, hop(): lax.ppermute(block, axis, [(i, (i + distance) % n) for i in range(n)])  30.9 us
    ppermute x16, waiting for transfers between devices, hop(): lax.ppermute(block, axis, [(i, (i + distance) % n) for i in range(n)])  28.7 us
    pallas_call x4, Pallas kernels, product(): pl.pallas_call(functools.partial(product_kernel, half), out_shape=[jax.Sh...  11.6 us
    ppermute x7, starting transfers between devices, swap(): return lax.ppermute(block, axis, [(0, 1), (1, 0)])  7.62 us
    ppermute x7, waiting for transfers between devices, swap(): return lax.ppermute(block, axis, [(0, 1), (1, 0)])  6.48 us
    pallas_call x4, Pallas kernels, attend(): pl.pallas_call(functools.partial(attend_kernel, plan, len(keys), state is...  6.41 us
    pallas_call x1, Pallas kernels, collect(): pl.pallas_call(collect_kernel, out_shape=jax.ShapeDtypeStruct((8, k, 2 *...  2.68 us
  transfers between devices with their start and end apart: 28, of which 14 were waited for; matrix products, arithmetic and copies ran while one was open for 4% of the time, Pallas kernels for 18%

profile of v3, /device:TPU:2, one launch (start us, length us, event | category | flops | bytes accessed | tf_op | source)
XLA Modules:
  0.0 109.9 jit_solution(3259517497848917148)
XLA Ops:
  0.0 1.2 %slice_bitcast_fusion = (bf16[336,512]{1,0:T(8,128)(2,1)S(1)}, bf16[336,512]{1,0:T(8,128)(2,1)S(1)}) fusion(bf16[1024,336]{0,1:T(8,128)(2,1)} %param.2), kind=kLoop, calls=%fused_computation.6 | loop fusion | bytes 1376256 | tf_op jit(solution)/shard_map/transpose | solution.py:325
  1.2 2.0 %collective-permute-start = (bf16[336,512]{1,0:T(8,128)(2,1)S(1)}, bf16[336,512]{1,0:T(8,128)(2,1)S(1)}, u32[]{:S(2)}, u32[]{:S(2)}) collective-permute-start(bf16[336,512]{1,0:T(8,128)(2,1)S(1)} %get-tuple-element.74.refs_0_), channel_id=1, source_target_pairs={{0,2},{2,4},{4,6},{6,8},{8,10},{10,12},{12,14},{14,0},{1,3},{3,5},... | collective-permute-start | bytes 1032200 | tf_op jit(solution)/shard_map/ppermute | solution.py:31
  3.2 4.0 %collective-permute-start.1 = (bf16[336,512]{1,0:T(8,128)(2,1)S(1)}, bf16[336,512]{1,0:T(8,128)(2,1)S(1)}, u32[]{:S(2)}, u32[]{:S(2)}) collective-permute-start(bf16[336,512]{1,0:T(8,128)(2,1)S(1)} %get-tuple-element.74.refs_0_), channel_id=1, source_target_pairs={{0,14},{2,0},{4,2},{6,4},{8,6},{10,8},{12,10},{14,12},{1,15},{3,1}... | collective-permute-start | bytes 1032200 | tf_op jit(solution)/shard_map/ppermute | solution.py:31
  7.2 0.5 collective-permute-start.3
  7.7 0.7 collective-permute-start.2
  8.4 0.1 collective-permute-start.6
  8.6 1.9 %fusion = (f32[1024,64]{1,0:T(8,128)S(1)}, f32[1024,64]{1,0:T(8,128)S(1)}, f32[1024,64]{1,0:T(8,128)S(1)}) fusion(f32[64]{0:T(128)S(1)} %multiply_power_fusion, f32[1024]{0:T(1024)S(1)} %add_convert_fusion), kind=kLoop, calls=%fused_computation.9 | loop fusion | flops 131072 | bytes 790784 | tf_op jit(solution)/shard_map/neg | solution.py:309
  10.5 1.3 %pad_maximum_fusion.1 = (f32[1024,128]{1,0:T(8,128)}, f32[1024,128]{1,0:T(8,128)}) fusion(f32[1024,64]{1,0:T(8,128)S(1)} %get-tuple-element.81, f32[1024,64]{1,0:T(8,128)S(1)} %get-tuple-element.80, f32[1024,64]{1,0:T(8,128)S(1)} %get-tuple-element.79), kind=kLoop, calls=%fused_computation.4 | loop fusion | flops 262144 | bytes 1835008 | tf_op jit(solution)/shard_map/concatenate | solution.py:309
  11.8 0.0 collective-permute-done.2
  11.8 3.2 %collective-permute-start.7 = (bf16[336,512]{1,0:T(8,128)(2,1)S(1)}, bf16[336,512]{1,0:T(8,128)(2,1)}, u32[]{:S(2)}, u32[]{:S(2)}) collective-permute-start(bf16[336,512]{1,0:T(8,128)(2,1)S(1)} %get-tuple-element.73.refs_0_), channel_id=1, source_target_pairs={{0,14},{2,0},{4,2},{6,4},{8,6},{10,8},{12,10},{14,12},{1,15},{3,1}... | collective-permute-start | bytes 1032200 | tf_op jit(solution)/shard_map/ppermute | solution.py:31
  15.0 0.4 collective-permute-done.3
  15.4 0.1 pad_maximum_fusion.refs_0_
  15.5 0.0 collective-permute-done.1.refs_2_
  15.5 0.1 collective-permute-start.4
  15.6 3.2 %collective-permute-start.5 = (bf16[336,512]{1,0:T(8,128)(2,1)S(1)}, bf16[336,512]{1,0:T(8,128)(2,1)S(1)}, u32[]{:S(2)}, u32[]{:S(2)}) collective-permute-start(bf16[336,512]{1,0:T(8,128)(2,1)S(1)} %collective-permute-done.1.refs_2_), channel_id=1, source_target_pairs={{0,14},{2,0},{4,2},{6,4},{8,6},{10,8},{12,10},{14,12},{1,15},{3,1}... | collective-permute-start | bytes 1032200 | tf_op jit(solution)/shard_map/ppermute | solution.py:31
  18.8 1.6 %collective-permute-start.10 = (bf16[2,336,512]{2,1,0:T(8,128)(2,1)S(1)}, bf16[2,336,512]{2,1,0:T(8,128)(2,1)S(1)}, u32[]{:S(2)}, u32[]{:S(2)}) collective-permute-start(bf16[2,336,512]{2,1,0:T(8,128)(2,1)S(1)} %pad_maximum_fusion.refs_0_), channel_id=1, source_target_pairs={{0,32},{32,64},{64,96},{96,0},{1,33},{33,65},{65,97},{97,1},{2,34}... | collective-permute-start | bytes 2064392 | tf_op jit(solution)/shard_map/ppermute | solution.py:31
  20.4 2.1 %collective-permute-done.6.refs_1_ = bf16[336,512]{1,0:T(8,128)(2,1)} collective-permute-done((bf16[336,512]{1,0:T(8,128)(2,1)S(1)}, bf16[336,512]{1,0:T(8,128)(2,1)}, u32[]{:S(2)}, u32[]{:S(2)}) %collective-permute-start.6) | collective-permute-done | bytes 344096 | tf_op jit(solution)/shard_map/ppermute | solution.py:31
  22.5 3.0 %collective-permute-start.11 = (bf16[2,336,512]{2,1,0:T(8,128)(2,1)S(1)}, bf16[2,336,512]{2,1,0:T(8,128)(2,1)S(1)}, u32[]{:S(2)}, u32[]{:S(2)}) collective-permute-start(bf16[2,336,512]{2,1,0:T(8,128)(2,1)S(1)} %pad_maximum_fusion.refs_0_), channel_id=1, source_target_pairs={{0,96},{32,0},{64,32},{96,64},{1,97},{33,1},{65,33},{97,65},{2,98}... | collective-permute-start | bytes 2064392 | tf_op jit(solution)/shard_map/ppermute | solution.py:31
  25.5 1.7 %collective-permute-done.4.refs_3_ = bf16[336,512]{1,0:T(8,128)(2,1)S(1)} collective-permute-done((bf16[336,512]{1,0:T(8,128)(2,1)S(1)}, bf16[336,512]{1,0:T(8,128)(2,1)S(1)}, u32[]{:S(2)}, u32[]{:S(2)}) %collective-permute-start.4) | collective-permute-done | bytes 344096 | tf_op jit(solution)/shard_map/ppermute | solution.py:31
  27.2 0.7 copy-done
  28.0 1.9 %collective-permute-start.8 = (bf16[336,512]{1,0:T(8,128)(2,1)}, bf16[336,512]{1,0:T(8,128)(2,1)}, u32[]{:S(2)}, u32[]{:S(2)}) collective-permute-start(bf16[336,512]{1,0:T(8,128)(2,1)} %collective-permute-done.6.refs_1_), channel_id=1, source_target_pairs={{0,2},{2,4},{4,6},{6,8},{8,10},{10,12},{12,14},{14,0},{1,3},{3,5},... | collective-permute-start | bytes 1032200 | tf_op jit(solution)/shard_map/ppermute | solution.py:31
  29.9 2.9 %collective-permute-start.9 = (bf16[336,512]{1,0:T(8,128)(2,1)}, bf16[336,512]{1,0:T(8,128)(2,1)}, u32[]{:S(2)}, u32[]{:S(2)}) collective-permute-start(bf16[336,512]{1,0:T(8,128)(2,1)} %collective-permute-done.7.refs_2_), channel_id=1, source_target_pairs={{0,14},{2,0},{4,2},{6,4},{8,6},{10,8},{12,10},{14,12},{1,15},{3,1}... | collective-permute-start | bytes 1032200 | tf_op jit(solution)/shard_map/ppermute | solution.py:31
  32.8 6.4 %collective-permute-done.8.refs_3_ = bf16[336,512]{1,0:T(8,128)(2,1)} collective-permute-done((bf16[336,512]{1,0:T(8,128)(2,1)}, bf16[336,512]{1,0:T(8,128)(2,1)}, u32[]{:S(2)}, u32[]{:S(2)}) %collective-permute-start.8) | collective-permute-done | bytes 344096 | tf_op jit(solution)/shard_map/ppermute | solution.py:31
  39.1 0.5 collective-permute-done.9.refs_4_
  39.7 0.0 collective-permute-done.10.refs_1_
  39.7 1.2 %collective-permute-done.11.refs_3_ = bf16[2,336,512]{2,1,0:T(8,128)(2,1)S(1)} collective-permute-done((bf16[2,336,512]{2,1,0:T(8,128)(2,1)S(1)}, bf16[2,336,512]{2,1,0:T(8,128)(2,1)S(1)}, u32[]{:S(2)}, u32[]{:S(2)}) %collective-permute-start.11) | collective-permute-done | bytes 688160 | tf_op jit(solution)/shard_map/ppermute | solution.py:31
  40.9 0.1 broadcast_select_fusion
  40.9 0.8 collective-permute-start.12
  41.7 3.0 %collective-permute-start.13 = (bf16[2,336,512]{2,1,0:T(8,128)(2,1)S(1)}, bf16[2,336,512]{2,1,0:T(8,128)(2,1)}, u32[]{:S(2)}, u32[]{:S(2)}) collective-permute-start(bf16[2,336,512]{2,1,0:T(8,128)(2,1)S(1)} %pad_maximum_fusion.refs_0_), channel_id=1, source_target_pairs={{0,16},{16,0},{1,17},{17,1},{2,18},{18,2},{3,19},{19,3},{4,20},{20... | collective-permute-start | bytes 2064392 | tf_op jit(solution)/shard_map/ppermute | solution.py:35
  44.8 1.1 %collective-permute-start.17 = (bf16[336,512]{1,0:T(8,128)(2,1)}, bf16[336,512]{1,0:T(8,128)(2,1)}, u32[]{:S(2)}, u32[]{:S(2)}) collective-permute-start(bf16[336,512]{1,0:T(8,128)(2,1)} %copy-done), channel_id=1, source_target_pairs={{0,2},{2,4},{4,6},{6,8},{8,10},{10,12},{12,14},{14,0},{1,3},{3,5},... | collective-permute-start | bytes 1032200 | tf_op jit(solution)/shard_map/ppermute | solution.py:31
  45.9 2.1 %collective-permute-start.18 = (bf16[336,512]{1,0:T(8,128)(2,1)}, bf16[336,512]{1,0:T(8,128)(2,1)}, u32[]{:S(2)}, u32[]{:S(2)}) collective-permute-start(bf16[336,512]{1,0:T(8,128)(2,1)} %copy-done.2), channel_id=1, source_target_pairs={{0,14},{2,0},{4,2},{6,4},{8,6},{10,8},{12,10},{14,12},{1,15},{3,1}... | collective-permute-start | bytes 1032200 | tf_op jit(solution)/shard_map/ppermute | solution.py:31
  48.0 0.0 collective-permute-start.14
  48.0 8.5 %collective-permute-done.17.refs_5_ = bf16[336,512]{1,0:T(8,128)(2,1)} collective-permute-done((bf16[336,512]{1,0:T(8,128)(2,1)}, bf16[336,512]{1,0:T(8,128)(2,1)}, u32[]{:S(2)}, u32[]{:S(2)}) %collective-permute-start.17) | collective-permute-done | bytes 344096 | tf_op jit(solution)/shard_map/ppermute | solution.py:31
  56.5 0.0 collective-permute-done.12.refs_2_
  56.5 0.5 collective-permute-start.15
  57.0 2.4 %collective-permute-start.22 = (bf16[336,512]{1,0:T(8,128)(2,1)}, bf16[336,512]{1,0:T(8,128)(2,1)S(1)}, u32[]{:S(2)}, u32[]{:S(2)}) collective-permute-start(bf16[336,512]{1,0:T(8,128)(2,1)} %collective-permute-done.9.refs_4_), channel_id=1, source_target_pairs={{0,14},{2,0},{4,2},{6,4},{8,6},{10,8},{12,10},{14,12},{1,15},{3,1}... | collective-permute-start | bytes 1032200 | tf_op jit(solution)/shard_map/ppermute | solution.py:31
  59.5 0.1 pad_add_fusion.where_ref
  59.5 1.1 fusion.2
  60.6 6.6 %collective-permute-done.22.refs_6_ = bf16[336,512]{1,0:T(8,128)(2,1)S(1)} collective-permute-done((bf16[336,512]{1,0:T(8,128)(2,1)}, bf16[336,512]{1,0:T(8,128)(2,1)S(1)}, u32[]{:S(2)}, u32[]{:S(2)}) %collective-permute-start.22) | collective-permute-done | bytes 344096 | tf_op jit(solution)/shard_map/ppermute | solution.py:31
  67.3 0.9 collective-permute-start.21
  68.2 2.3 %collective-permute-start.23 = (bf16[336,512]{1,0:T(8,128)(2,1)S(1)}, bf16[336,512]{1,0:T(8,128)(2,1)S(1)}, u32[]{:S(2)}, u32[]{:S(2)}) collective-permute-start(bf16[336,512]{1,0:T(8,128)(2,1)S(1)} %collective-permute-done.22.refs_6_), channel_id=1, source_target_pairs={{0,14},{2,0},{4,2},{6,4},{8,6},{10,8},{12,10},{14,12},{1,15},{3,1}... | collective-permute-start | bytes 1032200 | tf_op jit(solution)/shard_map/ppermute | solution.py:31
  70.5 2.7 %shard_map.28.weights_ref = bf16[8,336,1024]{2,1,0:T(8,128)(2,1)S(1)} custom-call(s32[3]{0:T(128)S(1)} %pad_add_fusion.where_ref, bf16[2,336,512]{2,1,0:T(8,128)(2,1)S(1)} %pad_maximum_fusion.refs_0_, bf16[2,336,512]{2,1,0:T(8,128)(2,1)S(1)} %collective-permute-done.10.refs_1_, bf16[2,336,512]{2,1,0:T(8,128)(2,1)} %collective-permute-done.12.refs_2_, ...), custom_call_target="tpu_custom_call" | custom-call | bytes 5505024 | tf_op jit(solution)/shard_map/pallas_call | solution.py:119
  73.2 2.8 %shard_map.29 = bf16[512,512]{1,0:T(8,128)(2,1)S(1)} custom-call(s32[1]{0:T(128)} %bitcast.1.z_ref, bf16[8,336,1024]{2,1,0:T(8,128)(2,1)S(1)} %shard_map.28.weights_ref, bf16[336,512]{1,0:T(8,128)(2,1)S(1)} %get-tuple-element.74.refs_0_, bf16[336,512]{1,0:T(8,128)(2,1)S(1)} %collective-permute-done.refs_1_, ...), custom_call_target="tpu_custom_call" | custom-call | flops 1409286144 | bytes 5505024 | tf_op jit(solution)/shard_map/pallas_call | solution.py:150
  76.1 0.1 collective-permute-start.20
  76.3 1.6 %collective-permute-done.21.refs_5_ = bf16[336,512]{1,0:T(8,128)(2,1)S(1)} collective-permute-done((bf16[336,512]{1,0:T(8,128)(2,1)}, bf16[336,512]{1,0:T(8,128)(2,1)S(1)}, u32[]{:S(2)}, u32[]{:S(2)}) %collective-permute-start.21) | collective-permute-done | bytes 344096 | tf_op jit(solution)/shard_map/ppermute | solution.py:31
  77.9 3.0 %shard_map.30 = (bf16[512,256]{1,0:T(8,128)(2,1)S(1)}, bf16[512,256]{1,0:T(8,128)(2,1)S(1)}) custom-call(s32[1]{0:T(128)} %bitcast.1.z_ref, bf16[8,336,1024]{2,1,0:T(8,128)(2,1)S(1)} %shard_map.28.weights_ref, bf16[336,512]{1,0:T(8,128)(2,1)S(1)} %get-tuple-element.73.refs_0_, bf16[336,512]{1,0:T(8,128)(2,1)} %collective-permute-done.6.refs_1_, ...), custom_call_target="tpu_custom_call" | custom-call | flops 1409286144 | bytes 5505024 | tf_op jit(solution)/shard_map/pallas_call | solution.py:150
  80.9 2.0 %collective-permute-start.25 = (bf16[512,256]{1,0:T(8,128)(2,1)S(1)}, bf16[512,256]{1,0:T(8,128)(2,1)S(1)}, u32[]{:S(2)}, u32[]{:S(2)}) collective-permute-start(bf16[512,256]{1,0:T(8,128)(2,1)S(1)} %get-tuple-element.56), channel_id=1, source_target_pairs={{0,1},{1,0},{2,3},{3,2},{4,5},{5,4},{6,7},{7,6},{8,9},{9,8},{10,11... | collective-permute-start | bytes 786440 | tf_op jit(solution)/shard_map/ppermute | solution.py:35
  82.9 2.8 %shard_map.31.keep_ref = f32[512,512]{1,0:T(8,128)S(1)} custom-call(s32[1]{0:T(128)} %bitcast.1.z_ref, bf16[8,336,1024]{2,1,0:T(8,128)(2,1)S(1)} %shard_map.28.weights_ref, bf16[336,512]{1,0:T(8,128)(2,1)S(1)} %get-tuple-element.74.refs_0_, bf16[336,512]{1,0:T(8,128)(2,1)S(1)} %collective-permute-done.refs_1_, ...), custom_call_target="tpu_custom_call" | custom-call | flops 1409286144 | bytes 5505024 | tf_op jit(solution)/shard_map/pallas_call | solution.py:150
  85.6 2.0 %collective-permute-start.24 = (bf16[512,256]{1,0:T(8,128)(2,1)S(1)}, bf16[512,256]{1,0:T(8,128)(2,1)S(1)}, u32[]{:S(2)}, u32[]{:S(2)}) collective-permute-start(bf16[512,256]{1,0:T(8,128)(2,1)S(1)} %get-tuple-element.60), channel_id=1, source_target_pairs={{0,1},{1,0},{2,3},{3,2},{4,5},{5,4},{6,7},{7,6},{8,9},{9,8},{10,11... | collective-permute-start | bytes 786440 | tf_op jit(solution)/shard_map/ppermute | solution.py:35
  87.6 3.0 %shard_map.32.keep_ref = f32[512,512]{1,0:T(8,128)S(1)} custom-call(s32[1]{0:T(128)} %bitcast.1.z_ref, bf16[8,336,1024]{2,1,0:T(8,128)(2,1)S(1)} %shard_map.28.weights_ref, bf16[336,512]{1,0:T(8,128)(2,1)S(1)} %get-tuple-element.73.refs_0_, bf16[336,512]{1,0:T(8,128)(2,1)} %collective-permute-done.6.refs_1_, ...), custom_call_target="tpu_custom_call" | custom-call | flops 1409286144 | bytes 5505024 | tf_op jit(solution)/shard_map/pallas_call | solution.py:150
  90.6 1.9 %collective-permute-done.20.sent_ref = bf16[512,512]{1,0:T(8,128)(2,1)S(1)} collective-permute-done((bf16[512,512]{1,0:T(8,128)(2,1)S(1)}, bf16[512,512]{1,0:T(8,128)(2,1)S(1)}, u32[]{:S(2)}, u32[]{:S(2)}) %collective-permute-start.20) | collective-permute-done | bytes 524320 | tf_op jit(solution)/shard_map/ppermute | solution.py:35
  92.5 0.3 shard_map.35
  92.9 1.9 %collective-permute-start.27 = (bf16[512,256]{1,0:T(8,128)(2,1)S(1)}, bf16[512,256]{1,0:T(8,128)(2,1)S(1)}, u32[]{:S(2)}, u32[]{:S(2)}) collective-permute-start(bf16[512,256]{1,0:T(8,128)(2,1)S(1)} %get-tuple-element.65.refs_1_), channel_id=1, source_target_pairs={{0,16},{16,32},{32,48},{48,64},{64,80},{80,96},{96,112},{112,128},... | collective-permute-start | bytes 786440 | tf_op jit(solution)/shard_map/ppermute | solution.py:340
  94.8 3.4 %collective-permute-done.25.sent_ref = bf16[512,256]{1,0:T(8,128)(2,1)S(1)} collective-permute-done((bf16[512,256]{1,0:T(8,128)(2,1)S(1)}, bf16[512,256]{1,0:T(8,128)(2,1)S(1)}, u32[]{:S(2)}, u32[]{:S(2)}) %collective-permute-start.25) | collective-permute-done | bytes 262176 | tf_op jit(solution)/shard_map/ppermute | solution.py:35
  98.2 0.2 shard_map.34.refs_1_.refs_0_
  98.3 1.9 %collective-permute-start.26 = (bf16[512,256]{1,0:T(8,128)(2,1)S(1)}, bf16[512,256]{1,0:T(8,128)(2,1)S(1)}, u32[]{:S(2)}, u32[]{:S(2)}) collective-permute-start(bf16[512,256]{1,0:T(8,128)(2,1)S(1)} %shard_map.34.refs_1_.refs_0_), channel_id=1, source_target_pairs={{0,16},{16,32},{32,48},{48,64},{64,80},{80,96},{96,112},{112,128},... | collective-permute-start | bytes 786440 | tf_op jit(solution)/shard_map/ppermute | solution.py:343
  100.3 1.2 %collective-permute-done.24.sent_ref = bf16[512,256]{1,0:T(8,128)(2,1)S(1)} collective-permute-done((bf16[512,256]{1,0:T(8,128)(2,1)S(1)}, bf16[512,256]{1,0:T(8,128)(2,1)S(1)}, u32[]{:S(2)}, u32[]{:S(2)}) %collective-permute-start.24) | collective-permute-done | bytes 262176 | tf_op jit(solution)/shard_map/ppermute | solution.py:35
  101.4 0.2 shard_map.33.q_ref
  101.6 1.6 %collective-permute-done.27.refs_0_ = bf16[512,256]{1,0:T(8,128)(2,1)S(1)} collective-permute-done((bf16[512,256]{1,0:T(8,128)(2,1)S(1)}, bf16[512,256]{1,0:T(8,128)(2,1)S(1)}, u32[]{:S(2)}, u32[]{:S(2)}) %collective-permute-start.27) | collective-permute-done | bytes 262176 | tf_op jit(solution)/shard_map/ppermute | solution.py:340
  103.3 1.6 %shard_map.37 = (f32[1024,128]{1,0:T(8,128)S(1)}, f32[1024,128]{1,0:T(8,128)S(1)}, f32[1024,128]{1,0:T(8,128)S(1)}) custom-call(s32[1]{0:T(128)} %bitcast.first_ref, bf16[512,256]{1,0:T(8,128)(2,1)S(1)} %get-tuple-element.69.q_ref, bf16[512,256]{1,0:T(8,128)(2,1)S(1)} %collective-permute-done.27.refs_0_, bf16[512,256]{1,0:T(8,128)(2,1)S(1)} %get-tuple-element.65.refs_1_), custom_call_target="tpu_custom_call" | custom-call | flops 402653184 | bytes 2097152 | tf_op jit(solution)/shard_map/pallas_call | solution.py:289
  104.9 1.1 shard_map.38.refs_4_
  106.0 2.0 %shard_map.36 = (f32[1024,128]{1,0:T(8,128)S(1)}, f32[1024,128]{1,0:T(8,128)S(1)}, f32[1024,128]{1,0:T(8,128)S(1)}) custom-call(s32[1]{0:T(128)} %bitcast.first_ref, bf16[512,256]{1,0:T(8,128)(2,1)S(1)} %shard_map.33.q_ref, bf16[512,256]{1,0:T(8,128)(2,1)S(1)} %collective-permute-done.27.refs_0_, bf16[512,256]{1,0:T(8,128)(2,1)S(1)} %shard_map.34.refs_1_.refs_0_), custom_call_target="tpu_custom_call" | custom-call | flops 469762048 | bytes 2097152 | tf_op jit(solution)/shard_map/pallas_call | solution.py:289
  108.0 0.2 collective-permute-done.26.refs_0_
  108.1 1.8 %shard_map.39 = bf16[1024,256]{1,0:T(8,128)(2,1)} custom-call(s32[1]{0:T(128)} %bitcast.first_ref, bf16[512,256]{1,0:T(8,128)(2,1)S(1)} %shard_map.33.q_ref, bf16[512,256]{1,0:T(8,128)(2,1)S(1)} %collective-permute-done.26.refs_0_, f32[1024,128]{1,0:T(8,128)S(1)} %get-tuple-element.66.refs_1_, f32[1024,128]{1,0:T(8,128)S(1)} %get-tuple-element.67.refs_2_, ...), custom_call_target="tpu_custom_call" | custom-call | flops 201326592 | bytes 2097152 | tf_op jit(solution)/shard_map/pallas_call | solution.py:289
  (27 shorter events, 0.1 us)
Async XLA Ops:
  0.0 15.0 %copy-start.5 = (bf16[336,512]{1,0:T(8,128)(2,1)S(1)}, bf16[336,512]{1,0:T(8,128)(2,1)}, u32[]{:S(2)}) copy-start(bf16[336,512]{1,0:T(8,128)(2,1)} %param.3) | copy-start | bytes 1032196
  1.2 14.3 %collective-permute-start = (bf16[336,512]{1,0:T(8,128)(2,1)S(1)}, bf16[336,512]{1,0:T(8,128)(2,1)S(1)}, u32[]{:S(2)}, u32[]{:S(2)}) collective-permute-start(bf16[336,512]{1,0:T(8,128)(2,1)S(1)} %get-tuple-element.74.refs_0_), channel_id=1, source_target_pairs={{0,2},{2,4},{4,6},{6,8},{8,10},{10,12},{12,14},{14,0},{1,3},{3,5},... | collective-permute-start | bytes 1032200 | tf_op jit(solution)/shard_map/ppermute | solution.py:31
  3.2 12.3 %collective-permute-start.1 = (bf16[336,512]{1,0:T(8,128)(2,1)S(1)}, bf16[336,512]{1,0:T(8,128)(2,1)S(1)}, u32[]{:S(2)}, u32[]{:S(2)}) collective-permute-start(bf16[336,512]{1,0:T(8,128)(2,1)S(1)} %get-tuple-element.74.refs_0_), channel_id=1, source_target_pairs={{0,14},{2,0},{4,2},{6,4},{8,6},{10,8},{12,10},{14,12},{1,15},{3,1}... | collective-permute-start | bytes 1032200 | tf_op jit(solution)/shard_map/ppermute | solution.py:31
  7.2 8.2 %collective-permute-start.3 = (bf16[336,512]{1,0:T(8,128)(2,1)}, bf16[336,512]{1,0:T(8,128)(2,1)S(1)}, u32[]{:S(2)}, u32[]{:S(2)}) collective-permute-start(bf16[336,512]{1,0:T(8,128)(2,1)} %param.3), channel_id=1, source_target_pairs={{0,128},{1,144},{16,129},{17,145},{128,0},{129,16},{144,1},{145,17... | collective-permute-start | bytes 1032200 | tf_op jit(solution)/shard_map/ppermute | solution.py:59
  7.7 4.0 %collective-permute-start.2 = (bf16[336,512]{1,0:T(8,128)(2,1)}, bf16[336,512]{1,0:T(8,128)(2,1)S(1)}, u32[]{:S(2)}, u32[]{:S(2)}) collective-permute-start(bf16[336,512]{1,0:T(8,128)(2,1)} %param.3), channel_id=1, source_target_pairs={{1,16},{16,1},{3,18},{18,3},{5,20},{20,5},{7,22},{22,7},{9,24},{24... | collective-permute-start | bytes 1032200 | tf_op jit(solution)/shard_map/ppermute | solution.py:52
  8.4 14.1 %collective-permute-start.6 = (bf16[336,512]{1,0:T(8,128)(2,1)S(1)}, bf16[336,512]{1,0:T(8,128)(2,1)}, u32[]{:S(2)}, u32[]{:S(2)}) collective-permute-start(bf16[336,512]{1,0:T(8,128)(2,1)S(1)} %get-tuple-element.73.refs_0_), channel_id=1, source_target_pairs={{0,2},{2,4},{4,6},{6,8},{8,10},{10,12},{12,14},{14,0},{1,3},{3,5},... | collective-permute-start | bytes 1032200 | tf_op jit(solution)/shard_map/ppermute | solution.py:31
  11.8 13.8 %collective-permute-start.7 = (bf16[336,512]{1,0:T(8,128)(2,1)S(1)}, bf16[336,512]{1,0:T(8,128)(2,1)}, u32[]{:S(2)}, u32[]{:S(2)}) collective-permute-start(bf16[336,512]{1,0:T(8,128)(2,1)S(1)} %get-tuple-element.73.refs_0_), channel_id=1, source_target_pairs={{0,14},{2,0},{4,2},{6,4},{8,6},{10,8},{12,10},{14,12},{1,15},{3,1}... | collective-permute-start | bytes 1032200 | tf_op jit(solution)/shard_map/ppermute | solution.py:31
  15.5 11.7 %collective-permute-start.4 = (bf16[336,512]{1,0:T(8,128)(2,1)S(1)}, bf16[336,512]{1,0:T(8,128)(2,1)S(1)}, u32[]{:S(2)}, u32[]{:S(2)}) collective-permute-start(bf16[336,512]{1,0:T(8,128)(2,1)S(1)} %collective-permute-done.refs_1_), channel_id=1, source_target_pairs={{0,2},{2,4},{4,6},{6,8},{8,10},{10,12},{12,14},{14,0},{1,3},{3,5},... | collective-permute-start | bytes 1032200 | tf_op jit(solution)/shard_map/ppermute | solution.py:31
  15.6 11.6 %collective-permute-start.5 = (bf16[336,512]{1,0:T(8,128)(2,1)S(1)}, bf16[336,512]{1,0:T(8,128)(2,1)S(1)}, u32[]{:S(2)}, u32[]{:S(2)}) collective-permute-start(bf16[336,512]{1,0:T(8,128)(2,1)S(1)} %collective-permute-done.1.refs_2_), channel_id=1, source_target_pairs={{0,14},{2,0},{4,2},{6,4},{8,6},{10,8},{12,10},{14,12},{1,15},{3,1}... | collective-permute-start | bytes 1032200 | tf_op jit(solution)/shard_map/ppermute | solution.py:31
  18.8 20.8 %collective-permute-start.10 = (bf16[2,336,512]{2,1,0:T(8,128)(2,1)S(1)}, bf16[2,336,512]{2,1,0:T(8,128)(2,1)S(1)}, u32[]{:S(2)}, u32[]{:S(2)}) collective-permute-start(bf16[2,336,512]{2,1,0:T(8,128)(2,1)S(1)} %pad_maximum_fusion.refs_0_), channel_id=1, source_target_pairs={{0,32},{32,64},{64,96},{96,0},{1,33},{33,65},{65,97},{97,1},{2,34}... | collective-permute-start | bytes 2064392 | tf_op jit(solution)/shard_map/ppermute | solution.py:31
  22.5 18.3 %collective-permute-start.11 = (bf16[2,336,512]{2,1,0:T(8,128)(2,1)S(1)}, bf16[2,336,512]{2,1,0:T(8,128)(2,1)S(1)}, u32[]{:S(2)}, u32[]{:S(2)}) collective-permute-start(bf16[2,336,512]{2,1,0:T(8,128)(2,1)S(1)} %pad_maximum_fusion.refs_0_), channel_id=1, source_target_pairs={{0,96},{32,0},{64,32},{96,64},{1,97},{33,1},{65,33},{97,65},{2,98}... | collective-permute-start | bytes 2064392 | tf_op jit(solution)/shard_map/ppermute | solution.py:31
  27.2 0.7 copy-start
  28.0 1.9 %copy-start.2 = (bf16[336,512]{1,0:T(8,128)(2,1)}, bf16[336,512]{1,0:T(8,128)(2,1)S(1)}, u32[]{:S(2)}) copy-start(bf16[336,512]{1,0:T(8,128)(2,1)S(1)} %collective-permute-done.5.refs_4_) | copy-start | bytes 1032196
  28.0 11.2 %collective-permute-start.8 = (bf16[336,512]{1,0:T(8,128)(2,1)}, bf16[336,512]{1,0:T(8,128)(2,1)}, u32[]{:S(2)}, u32[]{:S(2)}) collective-permute-start(bf16[336,512]{1,0:T(8,128)(2,1)} %collective-permute-done.6.refs_1_), channel_id=1, source_target_pairs={{0,2},{2,4},{4,6},{6,8},{8,10},{10,12},{12,14},{14,0},{1,3},{3,5},... | collective-permute-start | bytes 1032200 | tf_op jit(solution)/shard_map/ppermute | solution.py:31
  29.9 9.8 %collective-permute-start.9 = (bf16[336,512]{1,0:T(8,128)(2,1)}, bf16[336,512]{1,0:T(8,128)(2,1)}, u32[]{:S(2)}, u32[]{:S(2)}) collective-permute-start(bf16[336,512]{1,0:T(8,128)(2,1)} %collective-permute-done.7.refs_2_), channel_id=1, source_target_pairs={{0,14},{2,0},{4,2},{6,4},{8,6},{10,8},{12,10},{14,12},{1,15},{3,1}... | collective-permute-start | bytes 1032200 | tf_op jit(solution)/shard_map/ppermute | solution.py:31
  40.9 15.6 %collective-permute-start.12 = (bf16[2,336,512]{2,1,0:T(8,128)(2,1)S(1)}, bf16[2,336,512]{2,1,0:T(8,128)(2,1)}, u32[]{:S(2)}, u32[]{:S(2)}) collective-permute-start(bf16[2,336,512]{2,1,0:T(8,128)(2,1)S(1)} %broadcast_select_fusion), channel_id=1, source_target_pairs={{0,32},{16,112},{32,64},{48,16},{64,96},{80,48},{96,0},{112,80},{1... | collective-permute-start | bytes 2064392 | tf_op jit(solution)/shard_map/ppermute | solution.py:74
  41.7 17.7 %collective-permute-start.13 = (bf16[2,336,512]{2,1,0:T(8,128)(2,1)S(1)}, bf16[2,336,512]{2,1,0:T(8,128)(2,1)}, u32[]{:S(2)}, u32[]{:S(2)}) collective-permute-start(bf16[2,336,512]{2,1,0:T(8,128)(2,1)S(1)} %pad_maximum_fusion.refs_0_), channel_id=1, source_target_pairs={{0,16},{16,0},{1,17},{17,1},{2,18},{18,2},{3,19},{19,3},{4,20},{20... | collective-permute-start | bytes 2064392 | tf_op jit(solution)/shard_map/ppermute | solution.py:35
  44.8 11.7 %collective-permute-start.17 = (bf16[336,512]{1,0:T(8,128)(2,1)}, bf16[336,512]{1,0:T(8,128)(2,1)}, u32[]{:S(2)}, u32[]{:S(2)}) collective-permute-start(bf16[336,512]{1,0:T(8,128)(2,1)} %copy-done), channel_id=1, source_target_pairs={{0,2},{2,4},{4,6},{6,8},{8,10},{10,12},{12,14},{14,0},{1,3},{3,5},... | collective-permute-start | bytes 1032200 | tf_op jit(solution)/shard_map/ppermute | solution.py:31
  45.9 11.1 %collective-permute-start.18 = (bf16[336,512]{1,0:T(8,128)(2,1)}, bf16[336,512]{1,0:T(8,128)(2,1)}, u32[]{:S(2)}, u32[]{:S(2)}) collective-permute-start(bf16[336,512]{1,0:T(8,128)(2,1)} %copy-done.2), channel_id=1, source_target_pairs={{0,14},{2,0},{4,2},{6,4},{8,6},{10,8},{12,10},{14,12},{1,15},{3,1}... | collective-permute-start | bytes 1032200 | tf_op jit(solution)/shard_map/ppermute | solution.py:31
  48.0 20.2 %collective-permute-start.14 = (bf16[2,336,512]{2,1,0:T(8,128)(2,1)S(1)}, bf16[2,336,512]{2,1,0:T(8,128)(2,1)}, u32[]{:S(2)}, u32[]{:S(2)}) collective-permute-start(bf16[2,336,512]{2,1,0:T(8,128)(2,1)S(1)} %collective-permute-done.10.refs_1_), channel_id=1, source_target_pairs={{0,16},{16,0},{1,17},{17,1},{2,18},{18,2},{3,19},{19,3},{4,20},{20... | collective-permute-start | bytes 2064392 | tf_op jit(solution)/shard_map/ppermute | solution.py:35
  56.5 14.0 %collective-permute-start.16 = (bf16[2,336,512]{2,1,0:T(8,128)(2,1)S(1)}, bf16[2,336,512]{2,1,0:T(8,128)(2,1)}, u32[]{:S(2)}, u32[]{:S(2)}) collective-permute-start(bf16[2,336,512]{2,1,0:T(8,128)(2,1)S(1)} %collective-permute-done.11.refs_3_), channel_id=1, source_target_pairs={{0,16},{16,0},{1,17},{17,1},{2,18},{18,2},{3,19},{19,3},{4,20},{20... | collective-permute-start | bytes 2064392 | tf_op jit(solution)/shard_map/ppermute | solution.py:35
  56.5 14.0 %collective-permute-start.15 = (bf16[2,336,512]{2,1,0:T(8,128)(2,1)}, bf16[2,336,512]{2,1,0:T(8,128)(2,1)}, u32[]{:S(2)}, u32[]{:S(2)}) collective-permute-start(bf16[2,336,512]{2,1,0:T(8,128)(2,1)} %collective-permute-done.12.refs_2_), channel_id=1, source_target_pairs={{0,16},{16,0},{1,17},{17,1},{2,18},{18,2},{3,19},{19,3},{4,20},{20... | collective-permute-start | bytes 2064392 | tf_op jit(solution)/shard_map/ppermute | solution.py:35
  57.0 10.3 %collective-permute-start.22 = (bf16[336,512]{1,0:T(8,128)(2,1)}, bf16[336,512]{1,0:T(8,128)(2,1)S(1)}, u32[]{:S(2)}, u32[]{:S(2)}) collective-permute-start(bf16[336,512]{1,0:T(8,128)(2,1)} %collective-permute-done.9.refs_4_), channel_id=1, source_target_pairs={{0,14},{2,0},{4,2},{6,4},{8,6},{10,8},{12,10},{14,12},{1,15},{3,1}... | collective-permute-start | bytes 1032200 | tf_op jit(solution)/shard_map/ppermute | solution.py:31
  59.4 13.8 %collective-permute-start.19 = (bf16[336,512]{1,0:T(8,128)(2,1)}, bf16[336,512]{1,0:T(8,128)(2,1)S(1)}, u32[]{:S(2)}, u32[]{:S(2)}) collective-permute-start(bf16[336,512]{1,0:T(8,128)(2,1)} %collective-permute-done.17.refs_5_), channel_id=1, source_target_pairs={{0,2},{2,4},{4,6},{6,8},{8,10},{10,12},{12,14},{14,0},{1,3},{3,5},... | collective-permute-start | bytes 1032200 | tf_op jit(solution)/shard_map/ppermute | solution.py:31
  60.6 12.6 %copy-start.1 = (bf16[336,512]{1,0:T(8,128)(2,1)S(1)}, bf16[336,512]{1,0:T(8,128)(2,1)}, u32[]{:S(2)}) copy-start(bf16[336,512]{1,0:T(8,128)(2,1)} %copy-done) | copy-start | bytes 1032196
  60.6 12.6 %copy-start.3 = (bf16[336,512]{1,0:T(8,128)(2,1)S(1)}, bf16[336,512]{1,0:T(8,128)(2,1)}, u32[]{:S(2)}) copy-start(bf16[336,512]{1,0:T(8,128)(2,1)} %copy-done.2) | copy-start | bytes 1032196
  67.3 10.6 %collective-permute-start.21 = (bf16[336,512]{1,0:T(8,128)(2,1)}, bf16[336,512]{1,0:T(8,128)(2,1)S(1)}, u32[]{:S(2)}, u32[]{:S(2)}) collective-permute-start(bf16[336,512]{1,0:T(8,128)(2,1)} %collective-permute-done.8.refs_3_), channel_id=1, source_target_pairs={{0,2},{2,4},{4,6},{6,8},{8,10},{10,12},{12,14},{14,0},{1,3},{3,5},... | collective-permute-start | bytes 1032200 | tf_op jit(solution)/shard_map/ppermute | solution.py:31
  68.2 9.7 %collective-permute-start.23 = (bf16[336,512]{1,0:T(8,128)(2,1)S(1)}, bf16[336,512]{1,0:T(8,128)(2,1)S(1)}, u32[]{:S(2)}, u32[]{:S(2)}) collective-permute-start(bf16[336,512]{1,0:T(8,128)(2,1)S(1)} %collective-permute-done.22.refs_6_), channel_id=1, source_target_pairs={{0,14},{2,0},{4,2},{6,4},{8,6},{10,8},{12,10},{14,12},{1,15},{3,1}... | collective-permute-start | bytes 1032200 | tf_op jit(solution)/shard_map/ppermute | solution.py:31
  73.2 3.0 %copy-start.4 = (f32[1024,128]{1,0:T(8,128)S(1)}, f32[1024,128]{1,0:T(8,128)}, u32[]{:S(2)}) copy-start(f32[1024,128]{1,0:T(8,128)} %get-tuple-element.62) | copy-start | bytes 1572868
  76.1 16.5 %collective-permute-start.20 = (bf16[512,512]{1,0:T(8,128)(2,1)S(1)}, bf16[512,512]{1,0:T(8,128)(2,1)S(1)}, u32[]{:S(2)}, u32[]{:S(2)}) collective-permute-start(bf16[512,512]{1,0:T(8,128)(2,1)S(1)} %shard_map.29), channel_id=1, source_target_pairs={{0,1},{1,0},{2,3},{3,2},{4,5},{5,4},{6,7},{7,6},{8,9},{9,8},{10,11... | collective-permute-start | bytes 1572872 | tf_op jit(solution)/shard_map/ppermute | solution.py:35
  80.9 17.3 %collective-permute-start.25 = (bf16[512,256]{1,0:T(8,128)(2,1)S(1)}, bf16[512,256]{1,0:T(8,128)(2,1)S(1)}, u32[]{:S(2)}, u32[]{:S(2)}) collective-permute-start(bf16[512,256]{1,0:T(8,128)(2,1)S(1)} %get-tuple-element.56), channel_id=1, source_target_pairs={{0,1},{1,0},{2,3},{3,2},{4,5},{5,4},{6,7},{7,6},{8,9},{9,8},{10,11... | collective-permute-start | bytes 786440 | tf_op jit(solution)/shard_map/ppermute | solution.py:35
  85.6 15.8 %collective-permute-start.24 = (bf16[512,256]{1,0:T(8,128)(2,1)S(1)}, bf16[512,256]{1,0:T(8,128)(2,1)S(1)}, u32[]{:S(2)}, u32[]{:S(2)}) collective-permute-start(bf16[512,256]{1,0:T(8,128)(2,1)S(1)} %get-tuple-element.60), channel_id=1, source_target_pairs={{0,1},{1,0},{2,3},{3,2},{4,5},{5,4},{6,7},{7,6},{8,9},{9,8},{10,11... | collective-permute-start | bytes 786440 | tf_op jit(solution)/shard_map/ppermute | solution.py:35
  92.9 10.4 %collective-permute-start.27 = (bf16[512,256]{1,0:T(8,128)(2,1)S(1)}, bf16[512,256]{1,0:T(8,128)(2,1)S(1)}, u32[]{:S(2)}, u32[]{:S(2)}) collective-permute-start(bf16[512,256]{1,0:T(8,128)(2,1)S(1)} %get-tuple-element.65.refs_1_), channel_id=1, source_target_pairs={{0,16},{16,32},{32,48},{48,64},{64,80},{80,96},{96,112},{112,128},... | collective-permute-start | bytes 786440 | tf_op jit(solution)/shard_map/ppermute | solution.py:340
  98.3 9.8 %collective-permute-start.26 = (bf16[512,256]{1,0:T(8,128)(2,1)S(1)}, bf16[512,256]{1,0:T(8,128)(2,1)S(1)}, u32[]{:S(2)}, u32[]{:S(2)}) collective-permute-start(bf16[512,256]{1,0:T(8,128)(2,1)S(1)} %shard_map.34.refs_1_.refs_0_), channel_id=1, source_target_pairs={{0,16},{16,32},{32,48},{48,64},{64,80},{80,96},{96,112},{112,128},... | collective-permute-start | bytes 786440 | tf_op jit(solution)/shard_map/ppermute | solution.py:343
